TPU v7x, 32 devices: a whole 2x2x4 slice. The times are simulated.
32 devices in a mesh: dp: 8 (over z, y), fsdp: 4 (over x, core).
Axes of the slice: x: 2, y: 2, z: 4, core: 2. Of those that a mesh axis runs over, the one named last changes fastest.
Arguments:
- patches: bfloat16 [128, 324, 768], P(('dp', 'fsdp')), may hold values from -6 to 6
- groups: int32 [128], P(('dp', 'fsdp')), may hold values from 0 to 2, as said below
- labels: int32 [128], P(('dp', 'fsdp')), may hold values from 0 to 999
- wide_w: float32 [3, 192, 1536], P(None, None, ('dp', 'fsdp')), may hold values from -0.4375 to 0.4375
- down_w: float32 [3, 768, 192], P(None, ('dp', 'fsdp')), may hold values from -0.21875 to 0.21875
- plain: float32 [409408], P(('dp', 'fsdp'))
- wide_mom: float32 [3, 192, 1536], P(None, None, ('dp', 'fsdp')), may hold values from -9.1552734e-05 to 9.1552734e-05
- down_mom: float32 [3, 768, 192], P(None, ('dp', 'fsdp')), may hold values from -9.1552734e-05 to 9.1552734e-05
- plain_first: float32 [409408], P(('dp', 'fsdp')), may hold values from -9.1552734e-05 to 9.1552734e-05
- plain_second: float32 [409408], P(('dp', 'fsdp')), may hold values from 5.7586705e-12 to 2.3034681e-10
- basis_plain: float32 [64, 409408], P(None, ('dp', 'fsdp')), may hold values from -1 to 1, as said below
Outputs:
- loss_sum: float32 [], replicated
- removed_norm: float32 [], replicated
- grad_norm: float32 [], replicated
- wide_new: float32 [3, 192, 1536], P(None, None, ('dp', 'fsdp'))
- wide_mom_new: float32 [3, 192, 1536], P(None, None, ('dp', 'fsdp'))
- wide_copy: bfloat16 [3, 192, 1536], P(None, None, ('dp', 'fsdp'))
- down_new: float32 [3, 768, 192], P(None, ('dp', 'fsdp'))
- down_mom_new: float32 [3, 768, 192], P(None, ('dp', 'fsdp'))
- down_copy: bfloat16 [3, 768, 192], P(None, ('dp', 'fsdp'))
- plain_new: float32 [409408], P(('dp', 'fsdp'))
- plain_first_new: float32 [409408], P(('dp', 'fsdp'))
- plain_second_new: float32 [409408], P(('dp', 'fsdp'))
- plain_copy: bfloat16 [409408], P(('dp', 'fsdp'))
Inputs may be any that keep to these rules, and one draw needn't show every extreme that they name: `groups`: 0 for images of 101 tokens, 1 for 197, 2 for 325; every group occurs. `basis_plain`: the rows are orthonormal; every entry outside the final gain, the final shift and the head bias is zero.
All inputs are finite; a program needn't handle non-finite values.
Results may differ from a plain program's by a relative error of at most 0.01.
Values may be sent and summed in bfloat16 or wider, within the bound.
No kernel may reach another device: no remote copies, remote signals or barrier semaphores. Data moves between devices by JAX's collectives and lax.ppermute only.
A program may use at most 128 MiB of HBM per device.

v0:
```python
import jax
import jax.numpy as jnp
from jax import lax
from jax.sharding import PartitionSpec as P

D = 192
HEADS = 3
HD = 64
FF = 768
PATCH_DIM = 768
CLASSES = 1000
LAYERS = 3
SEQ = 325
LEN_MID = 197
LEN_SHORT = 101
STEP = 10


HIGH = lax.Precision.HIGHEST
NORM_EPS = 1e-06
CLIP_AT = 0.02
MUON_RATE = 0.3
ADAM_RATE = 0.05
BETA_ONE = 0.5
BETA_TWO = 0.95
DECAY_RATE = 0.01
ADAM_EPS = 1e-08
SHAPE_EPS = 1e-07
MASKED = -1e30


def pieces(flat_params):
    layout = [
        ("patch_w", PATCH_DIM * D, (PATCH_DIM, D)),
        ("head_w", D * CLASSES, (D, CLASSES)),
        ("cls_token", D, (D,)),
        ("patch_b", D, (D,)),
        ("position", SEQ * D, (SEQ, D)),
        ("layer_vec", LAYERS * (6 * D + FF), (LAYERS, 6 * D + FF)),
        ("final", 2 * D, (2, D)),
        ("head_b", CLASSES, (CLASSES,)),
    ]
    found = {}
    offset = 0
    for entry_name, entry_size, entry_shape in layout:
        found[entry_name] = flat_params[offset : offset + entry_size].reshape(entry_shape)
        offset += entry_size
    return found


def normalize(stream, gain, shift):
    average = jnp.mean(stream, -1, keepdims=True)
    centered = stream - average
    variance = jnp.mean(centered * centered, -1, keepdims=True)
    return centered * lax.rsqrt(variance + NORM_EPS) * gain + shift


def product(left, right):
    return jnp.einsum("ri,ij->rj", left, right, preferred_element_type=jnp.float32)


def left_grad(grad_low, right):
    return jnp.einsum("rj,ij->ri", grad_low, right, preferred_element_type=jnp.float32)


def right_grad(left, grad_low):
    return jnp.einsum("ri,rj->ij", left, grad_low, preferred_element_type=jnp.float32)


def layer_parts(stream, wide_full, down_full, vectors, key_valid):
    first_gain, first_shift, out_bias, second_gain, second_shift, down_bias = vectors[
        : 6 * D
    ].reshape(6, D)
    up_bias = vectors[6 * D :]
    batch_size = stream.shape[0]
    normed_one = normalize(stream, first_gain, first_shift).astype(jnp.bfloat16).reshape(-1, D)
    projected = product(normed_one, wide_full[:, : 3 * D]).reshape(batch_size, SEQ, 3 * D)
    queries = (
        (projected[..., :D] * HD ** (-0.5)).astype(jnp.bfloat16).reshape(batch_size, SEQ, HEADS, HD)
    )
    key_rows = projected[..., D : 2 * D].astype(jnp.bfloat16).reshape(batch_size, SEQ, HEADS, HD)
    value_rows = projected[..., 2 * D :].astype(jnp.bfloat16).reshape(batch_size, SEQ, HEADS, HD)
    scores = jnp.einsum("bqhd,bkhd->bhqk", queries, key_rows, preferred_element_type=jnp.float32)
    scores = jnp.where(key_valid[:, None, None, :] > 0, scores, MASKED)
    attention = jax.nn.softmax(scores, -1)
    attention_low = attention.astype(jnp.bfloat16)
    mixture = (
        jnp.einsum("bhqk,bkhd->bqhd", attention_low, value_rows, preferred_element_type=jnp.float32)
        .astype(jnp.bfloat16)
        .reshape(-1, D)
    )
    middle = (
        stream
        + product(mixture, wide_full[:, 3 * D : 4 * D]).reshape(batch_size, SEQ, D)
        + out_bias
    )
    normed_two = normalize(middle, second_gain, second_shift).astype(jnp.bfloat16).reshape(-1, D)
    upward = product(normed_two, wide_full[:, 4 * D :]) + up_bias
    active = jax.nn.gelu(upward, approximate=True).astype(jnp.bfloat16)
    output = middle + (product(active, down_full) + down_bias).reshape(batch_size, SEQ, D)
    return {
        "normed_one": normed_one,
        "queries": queries,
        "key_rows": key_rows,
        "value_rows": value_rows,
        "attention": attention,
        "attention_low": attention_low,
        "mixture": mixture,
        "middle": middle,
        "normed_two": normed_two,
        "upward": upward,
        "active": active,
        "output": output,
        "gains": (first_gain, first_shift, second_gain, second_shift),
    }


def layer_backward(grad_out, stream, wide_full, down_full, vectors, key_valid):
    saved = layer_parts(stream, wide_full, down_full, vectors, key_valid)
    first_gain, first_shift, second_gain, second_shift = saved["gains"]
    batch_size = stream.shape[0]
    out_rows = grad_out.reshape(-1, D)
    out_low = out_rows.astype(jnp.bfloat16)
    down_bias_grad = jnp.sum(out_rows, 0)
    down_grad = right_grad(saved["active"], out_low)
    active_grad = left_grad(out_low, down_full)
    upward_grad = jax.vjp(lambda value: jax.nn.gelu(value, approximate=True), saved["upward"])[1](
        active_grad
    )[0]
    upward_low = upward_grad.astype(jnp.bfloat16)
    up_bias_grad = jnp.sum(upward_grad, 0)
    up_grad = right_grad(saved["normed_two"], upward_low)
    normed_two_grad = left_grad(upward_low, wide_full[:, 4 * D :]).reshape(batch_size, SEQ, D)
    second_pull = jax.vjp(normalize, saved["middle"], second_gain, second_shift)[1]
    middle_grad, second_gain_grad, second_shift_grad = second_pull(normed_two_grad)
    middle_grad = middle_grad + grad_out
    middle_rows = middle_grad.reshape(-1, D)
    middle_low = middle_rows.astype(jnp.bfloat16)
    out_bias_grad = jnp.sum(middle_rows, 0)
    out_grad = right_grad(saved["mixture"], middle_low)
    mixture_low = (
        left_grad(middle_low, wide_full[:, 3 * D : 4 * D])
        .astype(jnp.bfloat16)
        .reshape(batch_size, SEQ, HEADS, HD)
    )
    attention_grad = jnp.einsum(
        "bqhd,bkhd->bhqk", mixture_low, saved["value_rows"], preferred_element_type=jnp.float32
    )
    value_grad = jnp.einsum(
        "bhqk,bqhd->bkhd", saved["attention_low"], mixture_low, preferred_element_type=jnp.float32
    )
    attention = saved["attention"]
    scores_low = (
        attention * (attention_grad - jnp.sum(attention * attention_grad, -1, keepdims=True))
    ).astype(jnp.bfloat16)
    query_grad = jnp.einsum(
        "bhqk,bkhd->bqhd", scores_low, saved["key_rows"], preferred_element_type=jnp.float32
    ) * HD ** (-0.5)
    key_grad = jnp.einsum(
        "bhqk,bqhd->bkhd", scores_low, saved["queries"], preferred_element_type=jnp.float32
    )
    projected_low = jnp.concatenate(
        [query_grad.reshape(-1, D), key_grad.reshape(-1, D), value_grad.reshape(-1, D)], 1
    ).astype(jnp.bfloat16)
    qkv_grad = right_grad(saved["normed_one"], projected_low)
    normed_one_grad = left_grad(projected_low, wide_full[:, : 3 * D]).reshape(batch_size, SEQ, D)
    first_pull = jax.vjp(normalize, stream, first_gain, first_shift)[1]
    stream_grad, first_gain_grad, first_shift_grad = first_pull(normed_one_grad)
    wide_grad = jnp.concatenate([qkv_grad, out_grad, up_grad], 1)
    vector_grad = jnp.concatenate(
        [
            first_gain_grad,
            first_shift_grad,
            out_bias_grad,
            second_gain_grad,
            second_shift_grad,
            down_bias_grad,
            up_bias_grad,
        ]
    )
    return (stream_grad + middle_grad, wide_grad, down_grad, vector_grad)


def orthogonalize(matrix):
    height, breadth = matrix.shape
    iterate = matrix.T if height > breadth else matrix
    iterate = iterate / (jnp.sqrt(jnp.sum(iterate * iterate)) + SHAPE_EPS)
    for iteration in range(5):
        gram_matrix = jnp.dot(iterate, iterate.T, precision=HIGH)
        polynomial = -4.775 * gram_matrix + 2.0315 * jnp.dot(
            gram_matrix, gram_matrix, precision=HIGH
        )
        iterate = 3.4445 * iterate + jnp.dot(polynomial, iterate, precision=HIGH)
    iterate = iterate.T if height > breadth else iterate
    return iterate * (MUON_RATE * 0.2 * max(height, breadth) ** 0.5)


def local(
    patches,
    groups,
    labels,
    wide_w,
    down_w,
    plain,
    wide_mom,
    down_mom,
    plain_first,
    plain_second,
    basis_plain,
):
    devices = lax.axis_size(("dp", "fsdp"))
    shard_index = lax.axis_index(("dp", "fsdp"))
    images = patches.shape[0]
    total_images = images * devices
    full_plain = lax.all_gather(plain, ("dp", "fsdp"), axis=0, tiled=True)
    found = pieces(full_plain)
    length = jnp.where(groups == 0, LEN_SHORT, jnp.where(groups == 1, LEN_MID, SEQ)).astype(
        jnp.int32
    )
    key_valid = (jnp.arange(SEQ, dtype=jnp.int32)[None, :] < length[:, None]).astype(jnp.int32)
    wide_low = wide_w.astype(jnp.bfloat16)
    down_low = down_w.astype(jnp.bfloat16)
    patch_rows = patches.reshape(-1, PATCH_DIM)
    patch_low = found["patch_w"].astype(jnp.bfloat16)
    embedded = product(patch_rows, patch_low).reshape(images, SEQ - 1, D) + found["patch_b"]
    leading = jnp.broadcast_to(found["cls_token"], (images, 1, D))
    stream = jnp.concatenate([leading, embedded], 1) + found["position"]

    def forward_step(stream_in, layer_in):
        wide_full, down_full = (
            lax.all_gather(layer_in[0], ("dp", "fsdp"), axis=1, tiled=True),
            lax.all_gather(layer_in[1], ("dp", "fsdp"), axis=0, tiled=True),
        )
        output = layer_parts(stream_in, wide_full, down_full, layer_in[2], key_valid)["output"]
        return (output, (stream_in,))

    last, saved = lax.scan(forward_step, stream, (wide_low, down_low, found["layer_vec"]))
    final_gain, final_shift = found["final"]
    final_rows = last[:, 0]
    final_low = normalize(final_rows, final_gain, final_shift).astype(jnp.bfloat16)
    head_low = found["head_w"].astype(jnp.bfloat16)
    logits = product(final_low, head_low) + found["head_b"]
    log_probs = jax.nn.log_softmax(logits, -1)
    onehot = (labels[:, None] == jnp.arange(CLASSES)[None, :]).astype(jnp.float32)
    loss_local = -jnp.sum(log_probs * onehot)
    logits_grad = (jnp.exp(log_probs) - onehot) / total_images
    logits_low = logits_grad.astype(jnp.bfloat16)
    head_grad = right_grad(final_low, logits_low)
    head_bias_grad = jnp.sum(logits_grad, 0)
    final_pull = jax.vjp(normalize, final_rows, final_gain, final_shift)[1]
    rows_grad, final_gain_grad, final_shift_grad = final_pull(left_grad(logits_low, head_low))
    grad_stream = jnp.zeros_like(last).at[:, 0].set(rows_grad)

    def backward_step(grad_out, layer_in):
        stream_in, wide_layer, down_layer, vectors = layer_in
        wide_full, down_full = (
            lax.all_gather(wide_layer, ("dp", "fsdp"), axis=1, tiled=True),
            lax.all_gather(down_layer, ("dp", "fsdp"), axis=0, tiled=True),
        )
        grad_in, wide_grad, down_grad, vector_grad = layer_backward(
            grad_out, stream_in, wide_full, down_full, vectors, key_valid
        )
        wide_shard, down_shard = (
            lax.psum_scatter(wide_grad, ("dp", "fsdp"), scatter_dimension=1, tiled=True),
            lax.psum_scatter(down_grad, ("dp", "fsdp"), scatter_dimension=0, tiled=True),
        )
        return (grad_in, (wide_shard, down_shard, vector_grad))

    backward_inputs = (saved[0], wide_low, down_low, found["layer_vec"])
    grad_stream, (wide_grads, down_grads, vector_grads) = lax.scan(
        backward_step, grad_stream, backward_inputs, reverse=True
    )
    embed_rows = grad_stream[:, 1:].reshape(-1, D)
    patch_grad = right_grad(patch_rows, embed_rows.astype(jnp.bfloat16))
    flat_grad = jnp.concatenate(
        [
            patch_grad.reshape(-1),
            head_grad.reshape(-1),
            jnp.sum(grad_stream[:, 0], 0),
            jnp.sum(embed_rows, 0),
            jnp.sum(grad_stream, 0).reshape(-1),
            vector_grads.reshape(-1),
            final_gain_grad,
            final_shift_grad,
            head_bias_grad,
        ]
    )
    flat_grad = jnp.concatenate(
        [flat_grad, jnp.zeros((full_plain.shape[0] - flat_grad.shape[0],), jnp.float32)]
    )
    plain_grads = lax.psum_scatter(flat_grad, ("dp", "fsdp"), scatter_dimension=0, tiled=True)
    coef_part = jnp.einsum("kp,p->k", basis_plain, plain_grads, precision=HIGH)
    coefficients, loss_sum = lax.psum((coef_part, loss_local), ("dp", "fsdp"))
    plain_grads = plain_grads - jnp.einsum("kp,k->p", basis_plain, coefficients, precision=HIGH)
    square_part = (
        jnp.sum(wide_grads * wide_grads)
        + jnp.sum(down_grads * down_grads)
        + jnp.sum(plain_grads * plain_grads)
    )
    square_sum = lax.psum(square_part, ("dp", "fsdp"))
    removed_norm = jnp.sqrt(jnp.sum(coefficients * coefficients))
    grad_norm = jnp.sqrt(square_sum)
    factor = CLIP_AT / jnp.maximum(grad_norm, CLIP_AT)
    wide_mom_new = BETA_ONE * wide_mom + wide_grads * factor
    down_mom_new = BETA_ONE * down_mom + down_grads * factor
    plain_grads = plain_grads * factor
    column_width = wide_mom.shape[2]
    row_width = down_mom.shape[1]
    wide_all, down_all = (
        lax.all_gather(wide_mom_new, ("dp", "fsdp"), axis=2, tiled=True),
        lax.all_gather(down_mom_new, ("dp", "fsdp"), axis=1, tiled=True),
    )
    bounds = ((0, 3 * D), (3 * D, 4 * D), (4 * D, 4 * D + FF))
    wide_list = []
    down_list = []
    for layer_index in range(LAYERS):
        wide_list.append(
            jnp.concatenate(
                [
                    orthogonalize(wide_all[layer_index, :, column_start:column_stop])
                    for column_start, column_stop in bounds
                ],
                1,
            )
        )
        down_list.append(orthogonalize(down_all[layer_index]))
    wide_update = lax.dynamic_slice_in_dim(
        jnp.stack(wide_list), shard_index * column_width, column_width, 2
    )
    down_update = lax.dynamic_slice_in_dim(
        jnp.stack(down_list), shard_index * row_width, row_width, 1
    )
    wide_new = wide_w - wide_update
    down_new = down_w - down_update
    first_new = BETA_ONE * plain_first + (1.0 - BETA_ONE) * plain_grads
    second_new = BETA_TWO * plain_second + (1.0 - BETA_TWO) * plain_grads * plain_grads
    first_hat = first_new / (1.0 - BETA_ONE**STEP)
    second_hat = second_new / (1.0 - BETA_TWO**STEP)
    plain_new = plain - ADAM_RATE * (
        first_hat / (jnp.sqrt(second_hat) + ADAM_EPS) + DECAY_RATE * plain
    )
    return (
        loss_sum,
        removed_norm,
        grad_norm,
        wide_new,
        wide_mom_new,
        wide_new.astype(jnp.bfloat16),
        down_new,
        down_mom_new,
        down_new.astype(jnp.bfloat16),
        plain_new,
        first_new,
        second_new,
        plain_new.astype(jnp.bfloat16),
    )


def solution(mesh):
    placed = (
        P(("dp", "fsdp"), None, None),
        P(("dp", "fsdp")),
        P(("dp", "fsdp")),
        P(None, None, ("dp", "fsdp")),
        P(None, ("dp", "fsdp"), None),
        P(("dp", "fsdp")),
        P(None, None, ("dp", "fsdp")),
        P(None, ("dp", "fsdp"), None),
        P(("dp", "fsdp")),
        P(("dp", "fsdp")),
        P(None, ("dp", "fsdp")),
    )
    return jax.shard_map(
        local,
        mesh=mesh,
        in_specs=placed,
        out_specs=(
            P(),
            P(),
            P(),
            P(None, None, ("dp", "fsdp")),
            P(None, None, ("dp", "fsdp")),
            P(None, None, ("dp", "fsdp")),
            P(None, ("dp", "fsdp"), None),
            P(None, ("dp", "fsdp"), None),
            P(None, ("dp", "fsdp"), None),
            P(("dp", "fsdp")),
            P(("dp", "fsdp")),
            P(("dp", "fsdp")),
            P(("dp", "fsdp")),
        ),
        check_vma=False,
    )
```

profile of v0, /device:TPU:0, one launch (start us, length us, event | category | flops | bytes accessed | tf_op | source)
XLA Modules:
  0.0 2110.4 jit_solution(3105364530461675385)
XLA Ops:
  12.1 135.8 %all-reduce.7.cloned.1.call-done = f32[409408]{0:T(1024)} async-done(((f32[409408]{0:T(1024)}), f32[409408]{0:T(1024)}) %all-reduce.7.cloned.1.call-update) | async-done | bytes 1637648
  167.7 408.4 %while.35 = (s32[]{:T(128)}, f32[4,325,192]{1,2,0:T(8,128)}, f32[3,4,325,192]{2,3,1,0:T(8,128)}, f32[3,1920]{1,0:T(4,128)}, bf16[3,192,48]{1,2,0:T(8,128)(2,1)S(...) while((s32[]{:T(128)}, f32[4,325,192]{1,2,0:T(8,128)}, ...), condition=%wide.region_7.8_spmd.clone, body=%wide.region_0.7_spmd.clone.sunk | while | flops 1497954048 | bytes 59301500 | solution.py:237
  172.5 43.8 %all-gather.13 = bf16[1,768,192]{2,1,0:T(8,128)(2,1)} all-gather(bf16[1,24,192]{2,1,0:T(8,128)(2,1)S(1)} %constant_dynamic-slice_fusion.13), channel_id=3, replica_groups=mesh['dp'=8,'fsdp'=4] {'dp','fsdp'}, dimensions={1}, use_global_device_ids=true | all-gather | bytes 304128 | tf_op jit(solution)/shard_map/while/body/eval_jaxpr/all_gather | solution.py:232
  216.3 41.4 %all-gather.12 = bf16[1,192,1536]{1,2,0:T(8,128)(2,1)} all-gather(bf16[1,192,48]{1,2,0:T(8,128)(2,1)S(1)} %constant_dynamic-slice_fusion.12), channel_id=2, replica_groups=mesh['dp'=8,'fsdp'=4] {'dp','fsdp'}, dimensions={2}, use_global_device_ids=true | all-gather | bytes 608256 | tf_op jit(solution)/shard_map/while/body/eval_jaxpr/all_gather | solution.py:231
  279.4 6.1 fusion.773
  295.3 4.1 convolution_add_fusion.56
  309.9 41.7 %all-gather.13 = bf16[1,768,192]{2,1,0:T(8,128)(2,1)} all-gather(bf16[1,24,192]{2,1,0:T(8,128)(2,1)S(1)} %constant_dynamic-slice_fusion.13), channel_id=3, replica_groups=mesh['dp'=8,'fsdp'=4] {'dp','fsdp'}, dimensions={1}, use_global_device_ids=true | all-gather | bytes 304128 | tf_op jit(solution)/shard_map/while/body/eval_jaxpr/all_gather | solution.py:232
  351.7 41.4 %all-gather.12 = bf16[1,192,1536]{1,2,0:T(8,128)(2,1)} all-gather(bf16[1,192,48]{1,2,0:T(8,128)(2,1)S(1)} %constant_dynamic-slice_fusion.12), channel_id=2, replica_groups=mesh['dp'=8,'fsdp'=4] {'dp','fsdp'}, dimensions={2}, use_global_device_ids=true | all-gather | bytes 608256 | tf_op jit(solution)/shard_map/while/body/eval_jaxpr/all_gather | solution.py:231
  414.7 6.1 fusion.773
  430.6 4.1 convolution_add_fusion.56
  445.3 41.7 %all-gather.13 = bf16[1,768,192]{2,1,0:T(8,128)(2,1)} all-gather(bf16[1,24,192]{2,1,0:T(8,128)(2,1)S(1)} %constant_dynamic-slice_fusion.13), channel_id=3, replica_groups=mesh['dp'=8,'fsdp'=4] {'dp','fsdp'}, dimensions={1}, use_global_device_ids=true | all-gather | bytes 304128 | tf_op jit(solution)/shard_map/while/body/eval_jaxpr/all_gather | solution.py:232
  487.0 41.4 %all-gather.12 = bf16[1,192,1536]{1,2,0:T(8,128)(2,1)} all-gather(bf16[1,192,48]{1,2,0:T(8,128)(2,1)S(1)} %constant_dynamic-slice_fusion.12), channel_id=2, replica_groups=mesh['dp'=8,'fsdp'=4] {'dp','fsdp'}, dimensions={2}, use_global_device_ids=true | all-gather | bytes 608256 | tf_op jit(solution)/shard_map/while/body/eval_jaxpr/all_gather | solution.py:231
  550.1 6.1 fusion.773
  566.0 4.1 convolution_add_fusion.56
  593.9 985.0 %while.36 = (s32[]{:T(128)}, f32[4,325,192]{1,2,0:T(8,128)}, f32[3,192,48]{2,1,0:T(8,128)}, f32[3,24,192]{2,1,0:T(8,128)}, f32[3,1920]{1,0:T(4,128)}, /*index=5*...) while((s32[]{:T(128)}, f32[4,325,192]{1,2,0:T(8,128)}, ...), condition=%wide.region_37.38_spmd.clone, body=%wide.region_16.37_spmd.clone.sunk | while | flops 4110707200 | bytes 270860800 | solution.py:270
  622.0 42.8 %all-gather.14 = bf16[1,192,1536]{1,2,0:T(8,128)(2,1)} all-gather(bf16[1,192,48]{1,2,0:T(8,128)(2,1)S(1)} %constant_dynamic-slice_fusion.14), channel_id=4, replica_groups=mesh['dp'=8,'fsdp'=4] {'dp','fsdp'}, dimensions={2}, use_global_device_ids=true | all-gather | bytes 608256 | tf_op jit(solution)/shard_map/while/body/eval_jaxpr/all_gather | solution.py:257
  687.0 6.1 fusion.808
  693.1 3.7 fusion.809
  714.0 37.7 %all-gather.15 = bf16[1,768,192]{2,1,0:T(8,128)(2,1)S(1)} all-gather(bf16[1,24,192]{2,1,0:T(8,128)(2,1)S(1)} %constant_dynamic-slice_fusion.15), channel_id=5, replica_groups=mesh['dp'=8,'fsdp'=4] {'dp','fsdp'}, dimensions={1}, use_global_device_ids=true | all-gather | bytes 304128 | tf_op jit(solution)/shard_map/while/body/eval_jaxpr/all_gather | solution.py:258
  751.6 5.5 fusion.812
  777.1 5.0 fusion.817
  782.1 4.1 multiply_reduce_fusion.43
  841.8 4.1 fusion.819
  847.2 85.0 %reduce-scatter.7.cloned.1.call-done = f32[48,192]{1,0:T(8,128)} async-done(((f32[1536,192]{1,0:T(8,128)}), f32[48,192]{1,0:T(8,128)}) %reduce-scatter.7.cloned.1.call-update) | async-done | bytes 36880 | tf_op jit(solution)/shard_map/while
  939.5 44.4 %all-gather.14 = bf16[1,192,1536]{1,2,0:T(8,128)(2,1)} all-gather(bf16[1,192,48]{1,2,0:T(8,128)(2,1)S(1)} %constant_dynamic-slice_fusion.14), channel_id=4, replica_groups=mesh['dp'=8,'fsdp'=4] {'dp','fsdp'}, dimensions={2}, use_global_device_ids=true | all-gather | bytes 608256 | tf_op jit(solution)/shard_map/while/body/eval_jaxpr/all_gather | solution.py:257
  1006.2 6.1 fusion.808
  1012.3 3.7 fusion.809
  1033.1 37.7 %all-gather.15 = bf16[1,768,192]{2,1,0:T(8,128)(2,1)S(1)} all-gather(bf16[1,24,192]{2,1,0:T(8,128)(2,1)S(1)} %constant_dynamic-slice_fusion.15), channel_id=5, replica_groups=mesh['dp'=8,'fsdp'=4] {'dp','fsdp'}, dimensions={1}, use_global_device_ids=true | all-gather | bytes 304128 | tf_op jit(solution)/shard_map/while/body/eval_jaxpr/all_gather | solution.py:258
  1070.8 5.5 fusion.812
  1096.2 5.0 fusion.817
  1101.2 4.1 multiply_reduce_fusion.43
  1161.0 4.1 fusion.819
  1166.4 84.9 %reduce-scatter.7.cloned.1.call-done = f32[48,192]{1,0:T(8,128)} async-done(((f32[1536,192]{1,0:T(8,128)}), f32[48,192]{1,0:T(8,128)}) %reduce-scatter.7.cloned.1.call-update) | async-done | bytes 36880 | tf_op jit(solution)/shard_map/while
  1258.6 44.4 %all-gather.14 = bf16[1,192,1536]{1,2,0:T(8,128)(2,1)} all-gather(bf16[1,192,48]{1,2,0:T(8,128)(2,1)S(1)} %constant_dynamic-slice_fusion.14), channel_id=4, replica_groups=mesh['dp'=8,'fsdp'=4] {'dp','fsdp'}, dimensions={2}, use_global_device_ids=true | all-gather | bytes 608256 | tf_op jit(solution)/shard_map/while/body/eval_jaxpr/all_gather | solution.py:257
  1325.3 6.1 fusion.808
  1331.4 3.7 fusion.809
  1352.2 37.7 %all-gather.15 = bf16[1,768,192]{2,1,0:T(8,128)(2,1)S(1)} all-gather(bf16[1,24,192]{2,1,0:T(8,128)(2,1)S(1)} %constant_dynamic-slice_fusion.15), channel_id=5, replica_groups=mesh['dp'=8,'fsdp'=4] {'dp','fsdp'}, dimensions={1}, use_global_device_ids=true | all-gather | bytes 304128 | tf_op jit(solution)/shard_map/while/body/eval_jaxpr/all_gather | solution.py:258
  1389.8 5.5 fusion.812
  1415.3 5.0 fusion.817
  1420.3 4.1 multiply_reduce_fusion.43
  1480.0 4.1 fusion.819
  1485.4 84.9 %reduce-scatter.7.cloned.1.call-done = f32[48,192]{1,0:T(8,128)} async-done(((f32[1536,192]{1,0:T(8,128)}), f32[48,192]{1,0:T(8,128)}) %reduce-scatter.7.cloned.1.call-update) | async-done | bytes 36880 | tf_op jit(solution)/shard_map/while
  1599.4 21.7 %concatenate.46 = f32[409408]{0:T(1024)} concatenate(f32[147456]{0:T(1024)} %reshape.642, f32[192000]{0:T(1024)} %reshape.643, f32[192]{0:T(256)} %slice_reduce_fusion.1, f32[192]{0:T(256)} %slice_reduce_fusion, f32[62400]{0:T(1024)S(1)} %reshape.644, f32[5760]{0:T(1024)S(1)} %reshape.645, f32[192]{0:T(256)} %get-tuple-element.495, f32[192]{0:T(256)} %get-tuple-element.499, ...), dimensions={0} | concatenate | bytes 3275264 | tf_op jit(solution)/shard_map/concatenate | solution.py:288
  1625.6 126.5 %all-reduce.9.cloned.1.call-done = f32[409408]{0:T(1024)} async-done(((f32[409408]{0:T(1024)}), f32[409408]{0:T(1024)}) %all-reduce.9.cloned.1.call-update) | async-done | bytes 1637648
  1755.7 39.9 %psum.22 = f32[64]{0:T(128)S(1)} all-reduce(f32[64]{0:T(128)S(1)} %convolution_bitcast_fusion), channel_id=1, replica_groups=mesh['dp'=8,'fsdp'=4] {'dp','fsdp'}, use_global_device_ids=true, to_apply=%region_45.46 | all-reduce | flops 64 | bytes 512 | tf_op jit(solution)/shard_map/psum | solution.py:293
  1799.4 40.0 %all-reduce.3 = (f32[]{:T(128)}, f32[]{:T(128)}) all-reduce(f32[]{:T(128)S(6)} %neg.12, f32[]{:T(128)S(6)} %add.861), channel_id=1, replica_groups=mesh['dp'=8,'fsdp'=4] {'dp','fsdp'}, use_global_device_ids=true, to_apply=%region_13.14 | all-reduce | flops 2 | bytes 16 | tf_op jit(solution)/shard_map/psum | solution.py:293
  1850.1 48.9 %all-gather.21.cloned.1.call-done = f32[3,768,192]{2,1,0:T(8,128)} async-done(((f32[3,24,192]{2,1,0:T(8,128)}), f32[3,768,192]{2,1,0:T(8,128)}) %all-gather.21.cloned.1.call-update) | async-done | bytes 1769488 | tf_op jit(solution)/shard_map/all_gather | solution.py:311
  1952.1 12.7 all-gather.19.cloned.1.call-done
  (970 shorter events, 756.0 us)
Async XLA Ops:
  7.2 1745.9 %copy-start = (f32[64,12794]{1,0:T(8,128)S(1)}, f32[64,12794]{1,0:T(8,128)}, u32[]{:S(2)}) copy-start(f32[64,12794]{1,0:T(8,128)} %param.27) | copy-start | bytes 9825796
  7.2 140.8 %all-reduce.7.cloned.1.call-start = ((), (), s32[]{:S(2)}) async-start(), calls=%async_computation.4 | async-start | bytes 3276800
  576.1 6.6 copy-start.74
  616.2 229.7 %reduce-scatter.9.cloned.1.call-start = ((), (), s32[]{:S(2)}) async-start(), calls=%async_computation.7 | async-start | bytes 811008 | tf_op jit(solution)/shard_map/while/body/eval_jaxpr/reduce_scatter | solution.py:265
  668.4 5.4 copy-start.1
  668.6 5.2 copy-start.38
  670.3 142.1 %copy-start.51 = (f32[1,192]{1,0:T(1,128)}, f32[1,192]{1,0:T(1,128)S(1)}, u32[]{:S(2)}) copy-start(f32[1,192]{1,0:T(1,128)S(1)} %get-tuple-element.811) | copy-start | bytes 2308 | tf_op jit(solution)/shard_map/while
  709.4 222.8 %reduce-scatter.7.cloned.1.call-start = ((), (), s32[]{:S(2)}) async-start(), calls=%async_computation.6 | async-start | bytes 1622016 | tf_op jit(solution)/shard_map/while
  710.1 41.5 %copy-start.26 = (bf16[1300,192]{0,1:T(8,128)(2,1)S(1)}, bf16[1300,192]{0,1:T(8,128)(2,1)}, u32[]{:S(2)}) copy-start(bf16[1300,192]{0,1:T(8,128)(2,1)} %convert_element_type.386) | copy-start | bytes 1497604 | tf_op jit(solution)/shard_map/while
  751.6 5.5 copy-start.12
  777.1 5.0 copy-start.22
  777.1 5.0 copy-start.24
  777.1 9.1 slice-start
  837.5 4.3 copy-start.39
  837.5 4.3 copy-start.54
  933.8 231.3 %reduce-scatter.9.cloned.1.call-start = ((), (), s32[]{:S(2)}) async-start(), calls=%async_computation.7 | async-start | bytes 811008 | tf_op jit(solution)/shard_map/while/body/eval_jaxpr/reduce_scatter | solution.py:265
  987.5 5.4 copy-start.1
  987.7 5.2 copy-start.38
  989.4 142.1 %copy-start.51 = (f32[1,192]{1,0:T(1,128)}, f32[1,192]{1,0:T(1,128)S(1)}, u32[]{:S(2)}) copy-start(f32[1,192]{1,0:T(1,128)S(1)} %get-tuple-element.811) | copy-start | bytes 2308 | tf_op jit(solution)/shard_map/while
  1028.5 222.8 %reduce-scatter.7.cloned.1.call-start = ((), (), s32[]{:S(2)}) async-start(), calls=%async_computation.6 | async-start | bytes 1622016 | tf_op jit(solution)/shard_map/while
  1029.3 41.5 %copy-start.26 = (bf16[1300,192]{0,1:T(8,128)(2,1)S(1)}, bf16[1300,192]{0,1:T(8,128)(2,1)}, u32[]{:S(2)}) copy-start(bf16[1300,192]{0,1:T(8,128)(2,1)} %convert_element_type.386) | copy-start | bytes 1497604 | tf_op jit(solution)/shard_map/while
  1070.8 5.5 copy-start.12
  1096.2 5.0 copy-start.22
  1096.2 5.0 copy-start.24
  1096.2 9.1 slice-start
  1156.6 4.3 copy-start.39
  1156.6 4.3 copy-start.54
  1252.9 231.2 %reduce-scatter.9.cloned.1.call-start = ((), (), s32[]{:S(2)}) async-start(), calls=%async_computation.7 | async-start | bytes 811008 | tf_op jit(solution)/shard_map/while/body/eval_jaxpr/reduce_scatter | solution.py:265
  1306.6 5.4 copy-start.1
  1306.8 5.2 copy-start.38
  1308.5 142.1 %copy-start.51 = (f32[1,192]{1,0:T(1,128)}, f32[1,192]{1,0:T(1,128)S(1)}, u32[]{:S(2)}) copy-start(f32[1,192]{1,0:T(1,128)S(1)} %get-tuple-element.811) | copy-start | bytes 2308 | tf_op jit(solution)/shard_map/while
  1347.6 222.8 %reduce-scatter.7.cloned.1.call-start = ((), (), s32[]{:S(2)}) async-start(), calls=%async_computation.6 | async-start | bytes 1622016 | tf_op jit(solution)/shard_map/while
  1348.3 41.5 %copy-start.26 = (bf16[1300,192]{0,1:T(8,128)(2,1)S(1)}, bf16[1300,192]{0,1:T(8,128)(2,1)}, u32[]{:S(2)}) copy-start(bf16[1300,192]{0,1:T(8,128)(2,1)} %convert_element_type.386) | copy-start | bytes 1497604 | tf_op jit(solution)/shard_map/while
  1389.8 5.5 copy-start.12
  1415.3 5.0 copy-start.22
  1415.3 5.0 copy-start.24
  1415.3 9.1 slice-start
  1420.3 4.2 slice-start.1
  1475.7 4.3 copy-start.39
  1475.7 4.3 copy-start.54
  1578.8 173.3 %all-reduce.9.cloned.1.call-start = ((), (), s32[]{:S(2)}) async-start(), calls=%async_computation.5 | async-start | bytes 3276800
  1594.3 5.1 copy-start.73
  1621.1 277.9 %all-gather.21.cloned.1.call-start = ((), (), s32[]{:S(2)}) async-start(), calls=%async_computation.3 | async-start | bytes 2433024 | tf_op jit(solution)/shard_map/all_gather | solution.py:311
  1795.6 46.4 %copy-start.60 = (f32[3,192,48]{1,2,0:T(8,128)S(1)}, f32[3,192,48]{1,2,0:T(8,128)}, u32[]{:S(2)}) copy-start(f32[3,192,48]{1,2,0:T(8,128)} %param.20) | copy-start | bytes 331780
  1841.7 123.1 %all-gather.19.cloned.1.call-start = ((), (), s32[]{:S(2)}) async-start(), calls=%async_computation.2 | async-start | bytes 4866048 | tf_op jit(solution)/shard_map/all_gather | solution.py:310
  1842.8 5.8 copy-start.63
  1986.4 9.4 slice-start.2
  1990.7 5.1 slice-start.3
  (133 other events, 290.7 us)
Sparse Core Ops, SparseCore 0:
  13.4 134.4 all-reduce.6
  709.5 91.6 reduce-scatter.8
  837.5 94.6 reduce-scatter.6
  1028.6 91.5 reduce-scatter.8
  1156.7 94.5 reduce-scatter.6
  1347.7 91.6 reduce-scatter.8
  1475.8 94.5 reduce-scatter.6
  1621.3 130.7 all-reduce.8
  1841.8 57.1 all-gather.20
  1902.3 62.4 all-gather.18
where the time goes:
time: 2120 us; the launch traced here: 2110 us
  waiting for transfers between devices  579 us (27%)
  blocking collectives  576 us (27%)
  local copies, waits for them, and re-layouts  425 us (20%)
  matrix products  335 us (16%)
  other arithmetic  133 us (6%)
  loops' own time  31 us (1%)
  between operations  30.8 us (1%)
    unnamed x6, waiting for transfers between devices  262 us
    while x9, waiting for transfers between devices  255 us
    all_gather x3, blocking collectives, backward_step(): lax.all_gather(wide_layer, ('dp', 'fsdp'), axis=1, tiled=True)  132 us
    all_gather x3, blocking collectives, forward_step(): lax.all_gather(layer_in[1], ('dp', 'fsdp'), axis=0, tiled=True)  127 us
    all_gather x3, blocking collectives, forward_step(): lax.all_gather(layer_in[0], ('dp', 'fsdp'), axis=1, tiled=True)  124 us
    all_gather x3, blocking collectives, backward_step(): lax.all_gather(down_layer, ('dp', 'fsdp'), axis=0, tiled=True)  113 us
    psum x2, blocking collectives, local(): coefficients, loss_sum = lax.psum((coef_part, loss_local), ('dp', 'fsdp'))  79.8 us
    while x294, local copies, waits for them, and re-layouts  52.3 us
  transfers between devices with their start and end apart: 10, of which 7 were waited for; matrix products, arithmetic and copies ran while one was open for 17% of the time, Pallas kernels for 0%

commit v1 on v0

v1 whole, which is shorter than its diff:
```python
import functools
import math

import jax
import jax.numpy as jnp
from jax import lax
from jax.experimental import pallas as pl
from jax.experimental.pallas import tpu as pltpu
from jax.sharding import PartitionSpec as P

D = 192
HEADS = 3
HD = 64
FF = 768
PATCH_DIM = 768
CLASSES = 1000
CLASSES_PAD = 1024
LAYERS = 3
SEQ = 325
PATCHES = SEQ - 1
LEN_MID = 197
LEN_SHORT = 101
BASIS = 64
STEP = 10
WIDE = 1536
ROWS_OUT = WIDE + FF

HEAD_AT = PATCH_DIM * D
CLS_AT = HEAD_AT + D * CLASSES
PATCH_B_AT = CLS_AT + D
POS_AT = PATCH_B_AT + D
VEC_AT = POS_AT + SEQ * D
VEC_LAYER = 6 * D + FF
FINAL_AT = VEC_AT + LAYERS * VEC_LAYER
HEAD_B_AT = FINAL_AT + 2 * D
USED = HEAD_B_AT + CLASSES
HEAD_ROWS = D * CLASSES // 128
BLOCK_PAD = 2 * D + CLASSES_PAD
PATCH_ROWS = HEAD_AT // 128
TAIL_ROW = CLS_AT // 128
TAIL_ROWS = FINAL_AT // 128 + 1 - TAIL_ROW

PACKED = ROWS_OUT * 3 // 2
MIDDLE_ROWS = 4096
FIRST_ROWS = 5632

TQ = 336
TK = 384
CLS_ROW = PATCHES

NORM_EPS = 1e-06
CLIP_AT = 0.02
MUON_RATE = 0.3
ADAM_RATE = 0.05
BETA_ONE = 0.5
BETA_TWO = 0.95
DECAY_RATE = 0.01
ADAM_EPS = 1e-08
SHAPE_EPS = 1e-07
MASKED = -1e30
GELU_C = math.sqrt(2.0 / math.pi)
GELU_K = 0.044715

F32 = jnp.float32
BF = jnp.bfloat16
AXES = ("dp", "fsdp")
NN = (((1,), (0,)), ((), ()))
NT = (((1,), (1,)), ((), ()))
TN = (((0,), (0,)), ((), ()))
VMEM_LIMIT = 60 * 1024 * 1024


def dot(a, b, how):
    return lax.dot_general(a, b, how, preferred_element_type=F32)


def lanes(shape):
    return lax.broadcasted_iota(jnp.int32, shape, len(shape) - 1)


def head_mask(h):
    lane = lanes((1, D))
    return jnp.where((lane >= h * HD) & (lane < (h + 1) * HD), 1.0, 0.0)


def norm_stats(x):
    mean = jnp.mean(x, -1, keepdims=True)
    centered = x - mean
    var = jnp.mean(centered * centered, -1, keepdims=True)
    rstd = lax.rsqrt(var + NORM_EPS)
    return centered * rstd, rstd


def norm_back(dn, xhat, rstd, gain):
    scaled = dn * gain
    m1 = jnp.mean(scaled, -1, keepdims=True)
    m2 = jnp.mean(scaled * xhat, -1, keepdims=True)
    return rstd * (scaled - m1 - xhat * m2)


def colsum(x):
    return jnp.sum(x, 0, keepdims=True)


def key_mask(length, rows):
    key = lanes((rows, TK))
    return ((key < length - 1) | (key == CLS_ROW)).astype(F32)


def softmax_rows(scores):
    top = jnp.max(scores, -1, keepdims=True)
    e = jnp.exp(scores - top)
    return e / jnp.sum(e, -1, keepdims=True)


def merge(a, b, shift):
    if shift == 0:
        return a
    lane = lanes(a.shape)
    return jnp.where(
        lane < 128 - shift, pltpu.roll(a, 128 - shift, 1), pltpu.roll(b, 128 - shift, 1)
    )


def flat_vec(flat, at, n):
    blocks = []
    for j in range(-(-n // 128)):
        q, r = divmod(at + 128 * j, 128)
        blocks.append(merge(flat[q : q + 1, :], flat[q + 1 : q + 2, :], r))
    row = blocks[0] if len(blocks) == 1 else jnp.concatenate(blocks, 1)
    return row[:, :n]


def unpack_flat(blocks, flat, tmp, devices, share):
    rows = blocks.shape[1]
    lane = lanes((rows, 128))
    for d in range(devices):
        q, r = divmod(d * share, 128)
        block = blocks[d]
        if r == 0:
            flat[q : q + rows, :] = block
            continue
        slot = d % 4
        tmp[slot, 8 : 8 + rows, :] = pltpu.roll(block, r, 1)
        tmp[slot, 7:8, :] = flat[q : q + 1, :]
        flat[q : q + rows, :] = jnp.where(
            lane >= r, tmp[slot, 8 : 8 + rows, :], tmp[slot, 7 : 7 + rows, :]
        )


def unpack_pairs(flat, row, pairs, out, out_at):
    a = flat[pl.ds(row, pairs, stride=3), :]
    b = flat[pl.ds(row + 1, pairs, stride=3), :]
    c = flat[pl.ds(row + 2, pairs, stride=3), :]
    out[0, pl.ds(out_at, pairs, stride=2), :] = a
    out[1, pl.ds(out_at, pairs, stride=2), :] = b
    out[0, pl.ds(out_at + 1, pairs, stride=2), :] = merge(b, c, 64)
    out[1, pl.ds(out_at + 1, pairs, stride=2), :] = pltpu.roll(c, 64, 1)


def rows192(ref, at, n):
    return jnp.concatenate([ref[0, at : at + n, :], ref[1, at : at + n, 0:64]], 1)


def pack_pairs(src, src_at, flat, row, pairs):
    a = src[0, pl.ds(src_at, pairs, stride=2), :]
    b = src[1, pl.ds(src_at, pairs, stride=2), :]
    c = src[0, pl.ds(src_at + 1, pairs, stride=2), :]
    e = src[1, pl.ds(src_at + 1, pairs, stride=2), :]
    lane = lanes(a.shape)
    c = pltpu.roll(c, 64, 1)
    flat[pl.ds(row, pairs, stride=3), :] = a
    flat[pl.ds(row + 1, pairs, stride=3), :] = jnp.where(lane < 64, b, c)
    flat[pl.ds(row + 2, pairs, stride=3), :] = jnp.where(lane < 64, c, pltpu.roll(e, 64, 1))


def unpack_head(flat, out):
    lane = lanes((12, 128))
    for rho in range(16):
        for k in range(8):
            q, r = divmod(1000 * rho + 128 * k, 128)
            a = flat[pl.ds(HEAD_AT // 128 + q, 12, stride=125), :]
            b = flat[pl.ds(HEAD_AT // 128 + q + 1, 12, stride=125), :]
            block = merge(a, b, r)
            if k == 7:
                block = jnp.where(lane < CLASSES - 896, block, 0.0)
            out[k, pl.ds(rho, 12, stride=16), :] = block


def pack_head(src, out):
    lane = lanes((12, 128))
    for j in range(125):
        rho, c = divmod(128 * j, 1000)
        k, s = divmod(c, 128)
        a = src[k, pl.ds(rho, 12, stride=16), :]
        if s:
            b = a
            if k < 7:
                b = src[k + 1, pl.ds(rho, 12, stride=16), :]
            a = merge(a, b, s)
        left = 1000 - c
        if left < 128:
            nxt = src[0, pl.ds(rho + 1, 12, stride=16), :]
            a = jnp.where(lane < left, a, pltpu.roll(nxt, left, 1))
        out[pl.ds(j, 12, stride=125), :] = a


FACTOR_FLOW = 24
FACTOR_DLOGITS = 26
FACTOR_BLOCKS = 34
EXACT = 13
EXACT_ROWS = 16


def put_factor(ref, block, value, images):
    for k in range(-(-value.shape[1] // 128)):
        part = value[0:images, 128 * k : 128 * (k + 1)].astype(F32)
        at = EXACT_ROWS + (block + k) * images
        ref[at : at + images, 0 : part.shape[1]] = part


def put_entries(ref, shift_rows, at, row, n):
    lane = lanes((1, 128))
    done = 0
    while done < n:
        q, r = divmod(at + done, 128)
        q = q + shift_rows
        take = min(128 - r, n - done)
        block, off = divmod(done, 128)
        piece = row[:, 128 * block : 128 * (block + 1)]
        if off + take > 128:
            piece = merge(piece, row[:, 128 * (block + 1) : 128 * (block + 2)], off)
            off = 0
        shift = (r - off) % 128
        if shift:
            piece = pltpu.roll(piece, shift, 1)
        if take < 128:
            piece = jnp.where((lane >= r) & (lane < r + take), piece, ref[q : q + 1, :])
        ref[q : q + 1, :] = piece
        done += take


def image_rows(i):
    return pl.ds(pl.multiple_of(i * TQ, 16), TQ)


def length_of(group):
    return jnp.where(group == 0, LEN_SHORT, jnp.where(group == 1, LEN_MID, SEQ))


def layer_vectors(flat, l):
    at = VEC_AT + l * VEC_LAYER
    six = [flat_vec(flat, at + k * D, D) for k in range(6)]
    return six, flat_vec(flat, at + 6 * D, FF)


def store_layer_grads(ref, parts):
    tails = []
    for at, g in parts:
        ref[at : at + g.shape[0], :] = g[:, 0:128]
        tails.append((at, g))
    half = ROWS_OUT // 2
    for at, g in tails:
        n = g.shape[0]
        low = max(0, min(n, half - at))
        if low > 0:
            ref[ROWS_OUT + at : ROWS_OUT + at + low, 0:64] = g[:low, 128:192]
        if low < n:
            start = at + low - half
            ref[ROWS_OUT + start : ROWS_OUT + start + n - low, 64:128] = g[low:, 128:192]


def half_rows(rows):
    return -(-rows // 8) * 8, -(-rows // 16) * 8


def unpack_weights(blocks, layers, column_width, row_width, asm, wt, dn):
    devices = blocks.shape[0]
    per_layer = column_width + row_width
    a_rows, h = half_rows(layers * per_layer)
    for l in range(layers):
        for d in range(devices):
            block = blocks[d].astype(F32)
            for at, n, to in (
                (l * per_layer, column_width, d * column_width),
                (l * per_layer + column_width, row_width, WIDE + d * row_width),
            ):
                asm[to : to + n, 0:128] = block[at : at + n]
                low = max(0, min(n, h - at))
                if low:
                    asm[to : to + low, 128:192] = block[a_rows + at : a_rows + at + low, 0:64]
                if low < n:
                    start = a_rows + at + low - h
                    asm[to + low : to + n, 128:192] = block[start : start + n - low, 64:128]
        wt[l] = asm[0:WIDE, :].astype(BF)
        dn[l] = asm[WIDE:ROWS_OUT, :].astype(BF)


def layer_forward(images, l, info, flat, wt, dn, gains, xin, xout, saved):
    mid, qs, ks, vs, mixs, acts, gps = saved
    masks = [head_mask(h).astype(BF) for h in range(HEADS)]
    (gain1, shift1, out_bias, gain2, shift2, down_bias), up_bias = layer_vectors(flat, l)
    for k, value in enumerate((gain1, shift1, gain2, shift2)):
        gains[k : k + 1, :] = value

    def layer(i, carry):
        rows = image_rows(i)
        x = xin[rows, :]
        xhat, _ = norm_stats(x)
        n1 = (xhat * gain1 + shift1).astype(BF)
        q = (dot(n1, wt[0, 0:D, :], NT) * HD ** (-0.5)).astype(BF)
        k = dot(n1, wt[0, D : 2 * D, :], NT).astype(BF)
        v = dot(n1, wt[0, 2 * D : 3 * D, :], NT).astype(BF)
        qs[rows, :] = q
        ks[i, 0:TQ, :] = k
        vs[i, 0:TQ, :] = v
        ks[i, TQ:TK, :] = jnp.zeros((TK - TQ, D), BF)
        vs[i, TQ:TK, :] = jnp.zeros((TK - TQ, D), BF)
        valid = key_mask(length_of(info[i]), 1)
        kk = ks[i]
        vv = vs[i]
        mix = None
        for h in range(HEADS):
            s = dot(q * masks[h], kk, NT)
            s = jnp.where(valid > 0, s, MASKED)
            p = softmax_rows(s).astype(BF)
            part = dot(p, vv * masks[h], NN)
            mix = part if mix is None else mix + part
        mix = mix.astype(BF)
        mixs[rows, :] = mix
        middle = x + dot(mix, wt[0, 3 * D : 4 * D, :], NT) + out_bias
        mid[rows, :] = middle
        xhat2, _ = norm_stats(middle)
        n2 = (xhat2 * gain2 + shift2).astype(BF)
        up = dot(n2, wt[0, 4 * D : WIDE, :], NT) + up_bias
        t = jnp.tanh(GELU_C * (up + GELU_K * (up * up * up)))
        half = 0.5 * (1.0 + t)
        act = (up * half).astype(BF)
        gps[rows, :] = half + 0.5 * up * (1.0 - t * t) * (
            GELU_C * (1.0 + 3.0 * GELU_K * (up * up))
        )
        acts[rows, :] = act
        xout[rows, :] = middle + dot(act, dn[0], NN) + down_bias
        return carry

    lax.fori_loop(0, images, layer, 0)


def start_kernel(devices, share, images, column_width, row_width, n_pieces, tops, info, where, *refs):
    pieces, top_pieces = refs[:n_pieces], refs[n_pieces : 2 * n_pieces]
    patches = refs[2 * n_pieces]
    x0, mid, qs, ks, vs, mixs, acts, gps, x1, gains, wt, dn, flat = refs[
        2 * n_pieces + 1 : 2 * n_pieces + 14
    ]
    blocks, weights, asm, tmp, pw, pos = refs[2 * n_pieces + 14 :]
    inner = pieces[0].shape[0]
    rows = blocks.shape[1]
    for k in range(n_pieces):
        for j in range(inner):
            d = where[k * inner + j]
            blocks[d] = pieces[k][j, 0:rows, :].astype(F32)
            weights[d] = pieces[k][j, rows:, :]
    top_inner = top_pieces[0].shape[0]
    for k in range(n_pieces):
        for j in range(top_inner):
            d = where[n_pieces * inner + k * top_inner + j]
            blocks[d] = blocks[d] + top_pieces[k][j].astype(F32)
    unpack_flat(blocks, flat, tmp, devices, share)
    unpack_weights(weights, 1, column_width, row_width, asm, wt, dn)
    unpack_pairs(flat, 0, PATCH_DIM // 2, pw, 0)
    unpack_pairs(flat, POS_AT // 128, SEQ // 2, pos, 7)
    last = flat_vec(flat, POS_AT + (SEQ - 1) * D, D)
    pos[0, 7 + SEQ - 1 : 7 + SEQ, :] = last[:, 0:128]
    pos[1, 7 + SEQ - 1 : 7 + SEQ, 0:64] = last[:, 128:192]
    cls = flat_vec(flat, CLS_AT, D)
    patch_b = flat_vec(flat, PATCH_B_AT, D)
    patch_low = rows192(pw, 0, PATCH_DIM).astype(BF)

    def embed(i, carry):
        base = pl.multiple_of(i * TQ, 16)
        e = dot(patches[i], patch_low, NN) + patch_b + rows192(pos, 8, PATCHES)
        x0[pl.ds(base, 320), :] = e[0:320]
        tail = jnp.concatenate(
            [e[320:324], cls + rows192(pos, 7, 1), jnp.zeros((TQ - SEQ, D), F32)], 0
        )
        x0[pl.ds(base + 320, 16), :] = tail
        return carry

    lax.fori_loop(0, images, embed, 0)
    layer_forward(
        images, 0, info, flat, wt, dn, gains, x0, x1, (mid, qs, ks, vs, mixs, acts, gps)
    )


def forward_kernel(
    total_images,
    images,
    column_width,
    row_width,
    n_pieces,
    info,
    where,
    flat,
    x1,
    *refs,
):
    pieces = refs[:n_pieces]
    mid, qs, ks, vs, mixs, acts, gps, gains, gstream, kv, factors, small, wt_all, dn_all = refs[
        n_pieces : n_pieces + 14
    ]
    (
        weights,
        asm,
        hw,
        n1buf,
        kbuf,
        vbuf,
        dkbuf,
        dvbuf,
        clsbuf,
        qcls,
        mixcls,
        dmixcls,
        dqcls,
        midgrad,
        n1low,
    ) = refs[n_pieces + 14 :]
    inner = pieces[0].shape[0]
    for k in range(n_pieces):
        for j in range(inner):
            weights[where[k * inner + j]] = pieces[k][j]
    unpack_weights(weights, 2, column_width, row_width, asm, wt_all, dn_all)
    unpack_head(flat, hw)
    factors[...] = jnp.zeros_like(factors)
    layer_forward(
        images,
        1,
        info,
        flat,
        wt_all,
        dn_all,
        gains,
        x1,
        n1buf,
        (mid, qs, ks, vs, mixs, acts, gps),
    )
    wt, dn = wt_all.at[1], dn_all.at[1]

    l = 2
    x2 = n1buf
    (gain1, shift1, out_bias, gain2, shift2, down_bias), up_bias = layer_vectors(flat, l)
    wk = wt[D : 2 * D, :]
    wv = wt[2 * D : 3 * D, :]
    clsbuf[...] = jnp.zeros_like(clsbuf)
    mixcls[...] = jnp.zeros_like(mixcls)
    kbuf[:, TQ:TK, :] = jnp.zeros((images, TK - TQ, D), BF)
    vbuf[:, TQ:TK, :] = jnp.zeros((images, TK - TQ, D), BF)

    def keys(i, carry):
        rows = image_rows(i)
        xhat, _ = norm_stats(x2[rows, :])
        n1 = (xhat * gain1 + shift1).astype(BF)
        kbuf[i, 0:TQ, :] = dot(n1, wk, NT).astype(BF)
        vbuf[i, 0:TQ, :] = dot(n1, wv, NT).astype(BF)
        clsbuf[pl.ds(i, 1), :] = x2[pl.ds(i * TQ + CLS_ROW, 1), :]
        return carry

    lax.fori_loop(0, images, keys, 0)
    xc = clsbuf[...]
    xhat1c, rstd1c = norm_stats(xc)
    n1c = (xhat1c * gain1 + shift1).astype(BF)
    qc = (dot(n1c, wt[0:D, :], NT) * HD ** (-0.5)).astype(BF)
    qcls[...] = qc.astype(F32)
    mask3 = jnp.concatenate([head_mask(h) for h in range(HEADS)] + [jnp.zeros((13, D), F32)], 0)

    def cls_probs(i):
        q3 = (qcls[pl.ds(i, 1), :] * mask3).astype(BF)
        s = dot(q3, kbuf[i], NT)
        s = jnp.where(key_mask(length_of(info[i]), 1) > 0, s, MASKED)
        return q3, softmax_rows(s)

    def attend(i, carry):
        q3, p = cls_probs(i)
        m = dot(p.astype(BF), vbuf[i], NN)
        mixcls[pl.ds(i, 1), :] = colsum(m * mask3)
        return carry

    lax.fori_loop(0, images, attend, 0)
    mixc = mixcls[...].astype(BF)
    midc = xc + dot(mixc, wt[3 * D : 4 * D, :], NT) + out_bias
    xhat2c, rstd2c = norm_stats(midc)
    n2c = (xhat2c * gain2 + shift2).astype(BF)
    upc = dot(n2c, wt[4 * D : WIDE, :], NT) + up_bias
    tc = jnp.tanh(GELU_C * (upc + GELU_K * (upc * upc * upc)))
    halfc = 0.5 * (1.0 + tc)
    actc = (upc * halfc).astype(BF)
    gpc = halfc + 0.5 * upc * (1.0 - tc * tc) * (GELU_C * (1.0 + 3.0 * GELU_K * (upc * upc)))
    outc = midc + dot(actc, dn[...], NN) + down_bias

    fgain = flat_vec(flat, FINAL_AT, D)
    fshift = flat_vec(flat, FINAL_AT + D, D)
    head_b = jnp.concatenate(
        [flat_vec(flat, HEAD_B_AT, CLASSES), jnp.zeros((1, CLASSES_PAD - CLASSES), F32)], 1
    )
    row16 = lax.broadcasted_iota(jnp.int32, (16, 1), 0)
    real = (row16 < images).astype(F32)
    xhatf, rstdf = norm_stats(outc)
    flow = (xhatf * fgain + fshift).astype(BF)
    head_low = jnp.concatenate([hw[k] for k in range(8)], 1).astype(BF)
    cls_lane = lanes((16, CLASSES_PAD))
    logits = dot(flow, head_low, NN) + head_b
    logits = jnp.where(cls_lane < CLASSES, logits, MASKED)
    top = jnp.max(logits, -1, keepdims=True)
    e = jnp.exp(logits - top)
    total = jnp.sum(e, -1, keepdims=True)
    labels = jnp.zeros((16, 1), jnp.int32)
    for i in range(images):
        labels = jnp.where(row16 == i, info[images + i], labels)
    onehot = (cls_lane == labels).astype(F32)
    picked = jnp.sum(jnp.where(cls_lane == labels, logits, 0.0), -1, keepdims=True)
    loss = jnp.sum((top + jnp.log(total) - picked) * real, 0, keepdims=True)
    dlogits = (e / total - onehot) * (real / total_images)
    dlow = dlogits.astype(BF)
    dflow = dot(dlow, head_low, NT)
    put_factor(factors, FACTOR_FLOW, flow, images)
    put_factor(factors, FACTOR_DLOGITS, dlow, images)
    small[...] = jnp.zeros_like(small)
    exact = [jnp.broadcast_to(loss, (1, 128))]
    head_bias_grad = colsum(dlogits)
    exact += [head_bias_grad[:, 128 * k : 128 * (k + 1)] for k in range(8)]
    for value in (colsum(dflow * xhatf), colsum(dflow)):
        value = jnp.concatenate([value, jnp.zeros((1, 64), F32)], 1)
        exact += [value[:, 0:128], value[:, 128:256]]
    for k, value in enumerate(exact):
        factors[k : k + 1, :] = value
    gout = norm_back(dflow, xhatf, rstdf, fgain) * real

    ol = gout.astype(BF)
    dact = dot(ol, dn[...], NT)
    dup = dact * gpc * real
    ul = dup.astype(BF)
    dn2 = dot(ul, wt[4 * D : WIDE, :], NN)
    dmid = norm_back(dn2, xhat2c, rstd2c, gain2) + gout
    ml = dmid.astype(BF)
    small[4:5, 0:FF] = colsum(dup)
    small[10:11, 0:D] = colsum(dmid)
    small[11:12, 0:D] = colsum(dn2 * xhat2c)
    small[12:13, 0:D] = colsum(dn2)
    small[13:14, 0:D] = colsum(gout)
    dmixcls[...] = dot(ml, wt[3 * D : 4 * D, :], NN).astype(BF).astype(F32)
    dqcls[...] = jnp.zeros_like(dqcls)

    def attend_back(i, carry):
        q3, p = cls_probs(i)
        dm3 = (dmixcls[pl.ds(i, 1), :] * mask3).astype(BF)
        dp = dot(dm3, vbuf[i], NT)
        dv = dot(p.astype(BF), dm3, TN)
        ds = (p * (dp - jnp.sum(p * dp, -1, keepdims=True))).astype(BF)
        dq = dot(ds, kbuf[i], NN)
        dk = dot(ds, q3, TN)
        rows = image_rows(i)
        dkbuf[rows, :] = dk[0:TQ].astype(BF)
        dvbuf[rows, :] = dv[0:TQ].astype(BF)
        dqcls[pl.ds(i, 1), :] = colsum(dq * mask3) * HD ** (-0.5)
        return carry

    lax.fori_loop(0, images, attend_back, 0)
    dql = dqcls[...].astype(BF)
    dn1c = dot(dql, wt[0:D, :], NN)
    midgrad[...] = dmid
    dqcls[...] = dn1c
    for k, value in enumerate((ol, n2c, ml, mixc, dql, n1c)):
        put_factor(factors, 2 * k, value, images)
    for k, value in enumerate((actc, ul)):
        put_factor(factors, 12 + 6 * k, value, images)

    def stream_back(i, carry):
        dgain, dshift = carry
        rows = image_rows(i)
        base = pl.multiple_of(i * TQ, 16)
        xhat, rstd = norm_stats(x2[rows, :])
        n1low[rows, :] = (xhat * gain1 + shift1).astype(BF)
        dkl = dkbuf[rows, :]
        dvl = dvbuf[rows, :]
        dn1 = dot(dkl, wk, NN) + dot(dvl, wv, NN)
        at_cls = lax.broadcasted_iota(jnp.int32, (TQ, 1), 0) == CLS_ROW
        dn1 = dn1 + jnp.where(at_cls, dqcls[pl.ds(i, 1), :], 0.0)
        gin = norm_back(dn1, xhat, rstd, gain1)
        gstream[rows, :] = gin + jnp.where(at_cls, midgrad[pl.ds(i, 1), :], 0.0)
        return (dgain + colsum(dn1 * xhat), dshift + colsum(dn1))

    zero_row = jnp.zeros((1, D), F32)
    dgain, dshift = lax.fori_loop(0, images, stream_back, (zero_row, zero_row))
    dwk = dot(dkbuf[...], n1low[...], TN)
    dwv = dot(dvbuf[...], n1low[...], TN)
    small[8:9, 0:D] = dgain
    small[9:10, 0:D] = dshift
    kv[0:D, :] = dwk[:, 0:128]
    kv[D : 2 * D, :] = dwv[:, 0:128]
    kv[2 * D :, 0:64] = dwk[:, 128:192]
    kv[2 * D :, 64:128] = dwv[:, 128:192]


def layer_back(
    images,
    info,
    x,
    mid,
    qs,
    ks,
    vs,
    mixs,
    acts,
    gps,
    gains_shifts,
    gout,
    wt,
    dn,
    gin,
    gt,
    vec,
    upb,
    olbuf,
    ulbuf,
    n2buf,
    mlbuf,
    n1buf,
    dqbuf,
    dkbuf,
    dvbuf,
):
    gain1, shift1, gain2, shift2 = gains_shifts
    masks = [head_mask(h).astype(BF) for h in range(HEADS)]
    vec[...] = jnp.zeros_like(vec)
    upb[...] = jnp.zeros_like(upb)

    def body(i, carry):
        rows = image_rows(i)
        go = gout[rows, :]
        ol = go.astype(BF)
        olbuf[rows, :] = ol
        dact = dot(ol, dn[0], NT)
        dup = dact * gps[rows, :]
        ul = dup.astype(BF)
        ulbuf[rows, :] = ul
        dn2 = dot(ul, wt[0, 4 * D : WIDE, :], NN)
        xhat2, rstd2 = norm_stats(mid[rows, :])
        n2buf[rows, :] = (xhat2 * gain2 + shift2).astype(BF)
        dmid = norm_back(dn2, xhat2, rstd2, gain2) + go
        ml = dmid.astype(BF)
        mlbuf[rows, :] = ml
        upb[0:1, :] += colsum(dup)
        vec[2:3, :] += colsum(dmid)
        vec[3:4, :] += colsum(dn2 * xhat2)
        vec[4:5, :] += colsum(dn2)
        vec[5:6, :] += colsum(go)
        dmix = dot(ml, wt[0, 3 * D : 4 * D, :], NN).astype(BF)
        valid = key_mask(length_of(info[i]), 1)
        q = qs[rows, :]
        kk = ks[i]
        vv = vs[i]
        dq = dk = dv = None
        for h in range(HEADS):
            qh = q * masks[h]
            dmh = dmix * masks[h]
            s = dot(qh, kk, NT)
            s = jnp.where(valid > 0, s, MASKED)
            p = softmax_rows(s)
            dp = dot(dmh, vv, NT)
            t = p * dp
            ds = (t - p * jnp.sum(t, -1, keepdims=True)).astype(BF)
            dv_h = dot(p.astype(BF), dmh, TN)
            dq_h = dot(ds, kk * masks[h], NN)
            dk_h = dot(ds, qh, TN)
            dq, dk, dv = (dq_h, dk_h, dv_h) if dq is None else (dq + dq_h, dk + dk_h, dv + dv_h)
        dql = (dq * HD ** (-0.5)).astype(BF)
        dkl = dk[0:TQ].astype(BF)
        dvl = dv[0:TQ].astype(BF)
        dqbuf[rows, :] = dql
        dkbuf[rows, :] = dkl
        dvbuf[rows, :] = dvl
        dn1 = (
            dot(dql, wt[0, 0:D, :], NN)
            + dot(dkl, wt[0, D : 2 * D, :], NN)
            + dot(dvl, wt[0, 2 * D : 3 * D, :], NN)
        )
        xhat1, rstd1 = norm_stats(x[rows, :])
        n1buf[rows, :] = (xhat1 * gain1 + shift1).astype(BF)
        vec[0:1, :] += colsum(dn1 * xhat1)
        vec[1:2, :] += colsum(dn1)
        gin[rows, :] = norm_back(dn1, xhat1, rstd1, gain1) + dmid
        return carry

    lax.fori_loop(0, images, body, 0)
    store_layer_grads(
        gt,
        [
            (0, dot(dqbuf[...], n1buf[...], TN)),
            (D, dot(dkbuf[...], n1buf[...], TN)),
            (2 * D, dot(dvbuf[...], n1buf[...], TN)),
            (3 * D, dot(mlbuf[...], mixs[...], TN)),
            (4 * D, dot(ulbuf[...], n2buf[...], TN)),
            (WIDE, dot(acts[...], olbuf[...], TN)),
        ],
    )


def share_halves(gt, keep, send, mine):
    half = keep.shape[0]
    keep[...] = gt[pl.ds(pl.multiple_of(mine * half, 8), half), :]
    send[...] = gt[pl.ds(pl.multiple_of((1 - mine) * half, 8), half), :]


def middle_kernel(images, info, *refs):
    (x, mid, qs, ks, vs, mixs, acts, gps, gains, gout, wt, dn, kv) = refs[:13]
    (gin, keep, send, vec, upb, gt) = refs[13:19]
    gs = tuple(gains[k : k + 1, :] for k in range(4))
    layer_back(
        images, info, x, mid, qs, ks, vs, mixs, acts, gps, gs, gout, wt, dn, gin, gt, vec, upb,
        *refs[19:],
    )
    gt[PACKED : PACKED + 3 * D, :] = kv[...]
    gt[PACKED + 3 * D :, :] = jnp.zeros((MIDDLE_ROWS - PACKED - 3 * D, 128), F32)
    share_halves(gt, keep, send, info[2 * images])


def first_kernel(images, info, *refs):
    (x, mid, qs, ks, vs, mixs, acts, gps, gains, gout, wt, dn) = refs[:12]
    (patches, small, vec1, upb1, keep, send) = refs[12:18]
    (gt, gin, vec, upb, pgrad, posgrad) = refs[18:24]
    gs = tuple(gains[k : k + 1, :] for k in range(4))
    layer_back(
        images, info, x, mid, qs, ks, vs, mixs, acts, gps, gs, gout, wt, dn, gin, gt, vec, upb,
        *refs[24:],
    )

    def pos_rows(at):
        return jnp.concatenate([posgrad[0, at : at + 1, :], posgrad[1, at : at + 1, :]], 1)

    pgrad[...] = jnp.zeros_like(pgrad)
    posgrad[...] = jnp.zeros_like(posgrad)

    def embed_back(i, carry):
        base = pl.multiple_of(i * TQ, 16)
        g = gin[image_rows(i), :]
        posgrad[0, 8 : 8 + TQ, :] += g[:, 0:128]
        posgrad[1, 8 : 8 + TQ, 0:64] += g[:, 128:192]
        gl = g.astype(BF)[0:PATCHES]
        pg = dot(patches[i], gl, TN)
        pgrad[0] += pg[:, 0:128]
        pgrad[1, :, 0:64] += pg[:, 128:192]
        return carry

    lax.fori_loop(0, images, embed_back, 0)
    cls_row = pos_rows(8 + CLS_ROW)
    patch_b = jnp.concatenate([colsum(posgrad[k, 8 : 8 + PATCHES, :]) for k in range(2)], 1)
    posgrad[0, 7:8, :] = cls_row[:, 0:128]
    posgrad[1, 7:8, :] = cls_row[:, 128:256]
    base = PACKED + PATCH_ROWS
    gt[base:, :] = jnp.zeros((FIRST_ROWS - base, 128), F32)
    pack_pairs(pgrad, 0, gt, PACKED, PATCH_DIM // 2)
    pack_pairs(posgrad, 7, gt, base + POS_AT // 128 - TAIL_ROW, SEQ // 2)
    put = functools.partial(put_entries, gt, base - TAIL_ROW)
    put(CLS_AT, cls_row, D)
    put(PATCH_B_AT, patch_b, D)
    put(POS_AT + (SEQ - 1) * D, pos_rows(7 + SEQ - 1), D)
    for layer in range(LAYERS):
        at = VEC_AT + layer * VEC_LAYER
        for k in range(6):
            if layer == 2:
                row = small[8 + k : 9 + k, 0:256]
            elif layer == 1:
                row = vec1[k : k + 1, :]
            else:
                row = vec[k : k + 1, :]
            if layer < 2:
                row = jnp.concatenate([row, jnp.zeros((1, 64), F32)], 1)
            put(at + k * D, row, D)
        row = small[4:5, 0:FF] if layer == 2 else (upb1 if layer == 1 else upb)[0:1, :]
        put(at + 6 * D, row, FF)
    share_halves(gt, keep, send, info[2 * images])


def parts(a):
    high = a.astype(BF)
    return high, (a - high.astype(F32)).astype(BF)


def parts_dot(a, b, how):
    return dot(a[0], b[0], how) + (dot(a[0], b[1], how) + dot(a[1], b[0], how))


def split_dot(a, b, how):
    return parts_dot(parts(a), parts(b), how)


def own_rows(ref, l, at, width):
    if width % 8 == 0:
        return ref[l, pl.ds(pl.multiple_of(at, 8), width), :]
    rows = -(-(width + 7) // 8) * 8
    base = pl.multiple_of((at // 8) * 8, 8)
    x = ref[l, pl.ds(base, rows), :]
    return pltpu.roll(x, lax.rem(rows - (at - base), rows), 0)[:width]


def coefficient_kernel(devices, gathered, basis, exact, extra):
    total = gathered[0]
    for d in range(1, devices):
        total = total + gathered[d]
    exact[...] = total
    c = split_dot(jnp.broadcast_to(block_row(exact), (8, BLOCK_PAD)), basis[...], NT)[0:1, :]
    extra[...] = jnp.zeros_like(extra)
    for k in range(3):
        high = c.astype(BF).astype(F32)
        extra[k : k + 1, 0:BASIS] = high
        c = c - high


def late_kernel(devices, images, gathered, g2, headflat, hg):
    rows = gathered.shape[0] // devices

    def factor(block, count):
        columns = []
        for b in range(block, block + count):
            parts = [
                gathered[pl.ds(EXACT_ROWS + b * images + i, devices, stride=rows), :]
                for i in range(images)
            ]
            columns.append(jnp.concatenate(parts, 0))
        return jnp.concatenate(columns, 1).astype(BF)

    ol, n2, ml, mix, dq, n1 = [factor(2 * k, 2)[:, 0:D] for k in range(6)]
    act, ul = factor(12, 6), factor(18, 6)
    g2[0:D, :] = dot(dq, n1, TN)
    g2[3 * D : 4 * D, :] = dot(ml, mix, TN)
    g2[4 * D : WIDE, :] = dot(ul, n2, TN)
    g2[WIDE:, :] = dot(act, ol, TN)
    flow = factor(FACTOR_FLOW, 2)[:, 0:D]
    for k in range(8):
        hg[k] = dot(flow, factor(FACTOR_DLOGITS + k, 1), TN)
    pack_head(hg, headflat)


def block_row(exact):
    pieces = [
        jnp.concatenate([exact[at : at + 1, :], exact[at + 1 : at + 2, 0:64]], 1) for at in (9, 11)
    ]
    pieces += [exact[1 + k : 2 + k, :] for k in range(8)]
    return jnp.concatenate(pieces, 1)


def unpack_layer(src, out, l, which):
    half = ROWS_OUT // 2
    for c in range(18):
        out[l, c * 128 : (c + 1) * 128, 0:128] = src[c * 128 : (c + 1) * 128, :].astype(F32)
    for c in range(9):
        g = src[ROWS_OUT + c * 128 : ROWS_OUT + (c + 1) * 128, :].astype(F32)
        out[l, c * 128 : (c + 1) * 128, 128:192] = g[:, 0:64]
        out[l, half + c * 128 : half + (c + 1) * 128, 128:192] = g[:, 64:128]


def square_rows(ref, start, stop, acc):
    step = 64
    for at in range(start, stop, step):
        g = ref[at : min(at + step, stop), :].astype(F32)
        g = g * g
        for lane in range(0, g.shape[1], 128):
            part = g[:, lane : lane + 128]
            rows = part.shape[0]
            part = jnp.sum(part.reshape(rows // 8, 8, part.shape[1]), 0)
            if part.shape[1] < 128:
                part = jnp.concatenate([part, jnp.zeros((8, 128 - part.shape[1]), F32)], 1)
            acc = acc + part
    return acc


def total_of(x):
    return jnp.sum(jnp.sum(x, 0, keepdims=True), 1, keepdims=True)


def muon_kernel(column_width, row_width, n_pieces, place, *refs):
    pieces = refs[:n_pieces]
    (
        g2,
        headflat,
        exact,
        basis,
        mom,
        wide_w,
        wide_mom,
        down_w,
        down_mom,
    ) = refs[n_pieces : n_pieces + 9]
    (
        wide_new,
        wide_mom_new,
        wide_copy,
        down_new,
        down_mom_new,
        down_copy,
        share_grad,
        scal,
        flat,
        mid_rows,
        first_rows,
        coef,
        gfull,
        mats,
        powers,
    ) = refs[n_pieces + 9 :]
    wide_at, down_at, mine = place[2], place[3], place[4]
    start = pl.multiple_of(place[0], 192)
    count = place[1]
    inner = pieces[0].shape[0]
    total_pieces = n_pieces * inner
    mr, fr = MIDDLE_ROWS // total_pieces, FIRST_ROWS // total_pieces

    for k in range(n_pieces):
        for z in range(inner):
            at = mine ^ (k * inner + z)
            mid_rows[pl.ds(pl.multiple_of(at * mr, 16), mr), :] = pieces[k][z, 0:mr, :]
            first_rows[pl.ds(pl.multiple_of(at * fr, 16), fr), :] = pieces[k][z, mr : mr + fr, :]
            coef[pl.ds(pl.multiple_of(at * 16, 16), 16), :] = pieces[k][
                z, mr + fr : mr + fr + 16, :
            ].astype(F32)
    unpack_layer(first_rows, gfull, 0, 0)
    unpack_layer(mid_rows, gfull, 1, 1)
    gfull[2, 0:D, :] = g2[0:D, :]
    gfull[2, 3 * D : ROWS_OUT, :] = g2[3 * D :, :]
    gfull[2, D : 3 * D, 0:128] = mid_rows[PACKED : PACKED + 2 * D, :].astype(F32)
    tail = mid_rows[PACKED + 2 * D : PACKED + 3 * D, :].astype(F32)
    gfull[2, D : 2 * D, 128:192] = tail[:, 0:64]
    gfull[2, 2 * D : 3 * D, 128:192] = tail[:, 64:128]

    base = PACKED + PATCH_ROWS
    flat[0:PATCH_ROWS, :] = first_rows[PACKED:base, :].astype(F32)
    flat[PATCH_ROWS : PATCH_ROWS + HEAD_ROWS, :] = headflat[0:HEAD_ROWS, :]
    flat[TAIL_ROW : TAIL_ROW + TAIL_ROWS, :] = first_rows[base : base + TAIL_ROWS, :].astype(F32)
    flat[TAIL_ROW + TAIL_ROWS :, :] = jnp.zeros(
        (flat.shape[0] - TAIL_ROW - TAIL_ROWS, 128), F32
    )
    block = block_row(exact)

    sums = jnp.zeros((16, 128), F32)
    for at in range(total_pieces):
        sums = sums + coef[16 * at : 16 * (at + 1), :]
    c = sums[0:1, :] + sums[1:2, :] + sums[2:3, :]
    acc = jnp.zeros((8, 128), F32)
    acc = square_rows(first_rows, 0, PACKED, acc)
    acc = square_rows(mid_rows, 0, PACKED + 3 * D, acc)
    acc = square_rows(g2, 0, D, acc)
    acc = square_rows(g2, 3 * D, ROWS_OUT, acc)
    acc = square_rows(flat, 0, flat.shape[0], acc)
    squares = total_of(acc) + total_of(jnp.where(lanes((1, BLOCK_PAD)) < 2 * D + CLASSES, block * block, 0.0))
    coef_square = jnp.sum(c * c, 1, keepdims=True)
    norm = jnp.sqrt(squares - coef_square)
    factor = CLIP_AT / jnp.maximum(norm, CLIP_AT)
    scal[...] = jnp.zeros_like(scal)
    for k, value in enumerate((norm, factor, jnp.sqrt(coef_square), exact[0:1, 0:1], c)):
        scal[k : k + 1, :] = jnp.broadcast_to(value, (1, 128))

    block = block - split_dot(
        jnp.broadcast_to(c[:, 0:BASIS], (8, BASIS)), basis[...], NN
    )[0:1, :]
    put_entries(flat, 0, FINAL_AT, block, 2 * D + CLASSES)
    rows = share_grad.shape[0]
    at, shift = place[5], place[6]
    base_row = pl.multiple_of((at // 8) * 8, 8)
    off = at - base_row
    window = flat[pl.ds(base_row, rows + 16), :]
    here = pltpu.roll(window, lax.rem(rows + 16 - off, rows + 16), 0)
    there = pltpu.roll(window, lax.rem(rows + 15 - off, rows + 16), 0)[0:rows]
    here = here[0:rows]
    back = lax.rem(128 - shift, 128)
    g = jnp.where(
        lanes((rows, 128)) < 128 - shift, pltpu.roll(here, back, 1), pltpu.roll(there, back, 1)
    )
    share_grad[...] = g * factor

    row = lax.broadcasted_iota(jnp.int32, (FF, 1), 0)
    sizes = []
    eye = (
        lax.broadcasted_iota(jnp.int32, (D, D), 0) == lax.broadcasted_iota(jnp.int32, (D, D), 1)
    ).astype(F32)
    for k in range(2 * LAYERS):
        l, which = divmod(k, 2)
        if which == 0:
            m = mom[pl.ds(start // column_width, FF // column_width), l, 0:column_width, :]
            m = BETA_ONE * m.reshape(FF, D) + factor * gfull[l, pl.ds(start, FF), :]
            m = jnp.where(row < count, m, 0.0)
        else:
            m = BETA_ONE * mom[:, l, column_width:, :].reshape(FF, D) + factor * gfull[l, WIDE:ROWS_OUT, :]
        size = 1.0 / (jnp.sqrt(total_of(m * m)) + SHAPE_EPS)
        sizes.append(size)
        x = m * size
        mats[k] = split_dot(x, x, TN)
        powers[k] = eye

    def polynomial(k):
        a = parts(mats[k])
        b = parts_dot(a, a, NN)
        return a, 3.4445 * eye - 4.775 * mats[k] + 2.0315 * b

    def step(it, carry):
        polys = [polynomial(k) for k in range(2 * LAYERS)]
        ps = [parts(p) for _, p in polys]
        ts = [parts(parts_dot(p, a, NN)) for (a, _), p in zip(polys, ps)]
        for k in range(2 * LAYERS):
            mats[k] = parts_dot(ts[k], ps[k], NN)
            powers[k] = parts_dot(ps[k], parts(powers[k]), NN)
        return carry

    lax.fori_loop(0, 4, step, 0)
    side = jnp.where(count == 4 * D, 768.0, jnp.where(count == 3 * D, 576.0, 192.0))
    rate = jnp.sqrt(jnp.full((1, 1), 1.0, F32) * side) * (MUON_RATE * 0.2)
    for k in range(2 * LAYERS):
        l, which = divmod(k, 2)
        _, p = polynomial(k)
        q = parts_dot(parts(p), parts(powers[k]), NN)
        if which == 0:
            g = own_rows(gfull, l, wide_at, column_width)
            own = BETA_ONE * wide_mom[l] + factor * g
            update = split_dot(own * sizes[k], q, NN)
            new = wide_w[l] - rate * update
            wide_mom_new[l] = own
            wide_new[l] = new
            wide_copy[l] = new.astype(BF)
        else:
            g = own_rows(gfull, l, down_at, row_width)
            own = BETA_ONE * down_mom[l] + factor * g
            update = split_dot(own * sizes[k], q, NN)
            new = down_w[l] - (MUON_RATE * 0.2 * FF**0.5) * update
            down_mom_new[l] = own
            down_new[l] = new
            down_copy[l] = new.astype(BF)


def cost(micros):
    return pl.CostEstimate(
        flops=int(micros * 1.15e9), bytes_accessed=int(micros * 1e6), transcendentals=0
    )


def pad_rows(x, rows):
    return jnp.pad(x, (0, rows * 128 - x.shape[0])).reshape(rows, 128)


def pack_shard(wide_t, down):
    rows = jnp.concatenate([wide_t, down], 1)
    rows = rows.reshape(-1, D).astype(BF)
    a_rows, h = half_rows(rows.shape[0])
    head = jnp.pad(rows[:, :128], ((0, a_rows - rows.shape[0]), (0, 0)))
    tail = jnp.pad(rows[:, 128:], ((0, 2 * h - rows.shape[0]), (0, 0)))
    tail = jnp.concatenate([tail[:h], tail[h:]], 1)
    fill = -(a_rows + h) % 16
    return jnp.concatenate([head, tail] + ([jnp.zeros((fill, 128), BF)] if fill else []), 0)


def stage_masks(stages):
    masks = [0]
    for low, width in reversed(stages):
        masks = [a ^ (m << low) for m in range(1 << width) for a in masks]
    return masks


def gather_stages(arrays, stages, devices, apart=2):
    for depth in reversed(range(len(stages))):
        low, width = stages[depth]
        got = [swap(x, m << low, devices) for m in range(1, 1 << width) for x in arrays]
        arrays = arrays + got
        if depth >= apart:
            arrays = [jnp.concatenate(arrays, 0)]
    return arrays


def swap(x, mask, devices):
    return lax.ppermute(x, AXES, [(i, i ^ mask) for i in range(devices)])


def local(
    patches,
    groups,
    labels,
    wide_w,
    down_w,
    plain,
    wide_mom,
    down_mom,
    plain_first,
    plain_second,
    basis_plain,
):
    devices = lax.axis_size(AXES)
    bits = devices.bit_length() - 1
    me = lax.axis_index(AXES).astype(jnp.int32)
    images = patches.shape[0]
    share = plain.shape[0]
    column_width = wide_w.shape[2]
    row_width = down_w.shape[1]
    vmem = pl.BlockSpec(memory_space=pltpu.VMEM)
    smem = pl.BlockSpec(memory_space=pltpu.SMEM)
    params = pltpu.CompilerParams(vmem_limit_bytes=VMEM_LIMIT)
    S = jax.ShapeDtypeStruct

    number_of = [(0, 1), (1, 2), (3, 2)]
    stages = number_of + ([(5, 2), (7, 1)] if bits == 8 else [(b, 1) for b in range(5, bits)])

    wide_t = jnp.transpose(wide_w, (0, 2, 1))
    plain_rows = -(-(share + 127) // 2048) * 16
    rows = plain_rows
    plain_block = pad_rows(plain, plain_rows)
    high = lax.reduce_precision(plain_block, 8, 7)
    low_half = (plain_block - high).astype(BF)
    shard_one = jnp.concatenate([high.astype(BF), pack_shard(wide_t[:1], down_w[:1])], 0)
    shard_two = pack_shard(wide_t[1:], down_w[1:])

    top = 3 * devices // 4
    if bits == 5 and top * share <= CLS_AT:
        low_all = None
        for m in range(1, 4):
            got = lax.ppermute(
                low_half, AXES, [(i, i ^ (m << 3)) for i in range(top, devices)]
            )
            low_all = got if low_all is None else low_all + got
        low_all = jnp.where(me >= top, low_half, low_all)[None]
        top_arrays = gather_stages([low_all], number_of[:2], devices)
        top_where = [top | ((me ^ m) & 7) for m in stage_masks(number_of[:2])]
    else:
        top_arrays = gather_stages([low_half[None]], stages, devices)
        top_where = [me ^ m for m in stage_masks(stages)]
    one = gather_stages([shard_one[None]], stages[1:], devices, 1)
    two = gather_stages([shard_two[None]], stages[2:], devices, 0)
    one, two = lax.optimization_barrier((one, two))
    pieces_one = gather_stages(one, stages[:1], devices)
    two = gather_stages(two, stages[1:2], devices)
    where_one = [me ^ m for m in stage_masks(stages)]

    lead = jnp.clip(FINAL_AT - me * share + BLOCK_PAD, 0, share + BLOCK_PAD)
    basis_block = lax.dynamic_slice(
        jnp.pad(basis_plain, ((0, 0), (BLOCK_PAD, BLOCK_PAD))), (0, lead), (BASIS, BLOCK_PAD)
    )

    info = jnp.concatenate([groups, labels, (me & 1)[None]]).astype(jnp.int32)
    flat_rows = -(-((devices - 1) * share // 128 + rows + 8) // 8) * 8
    n = images * TQ
    saved = [
        S((n, D), F32),
        S((n, D), BF),
        S((images, TK, D), BF),
        S((images, TK, D), BF),
        S((n, D), BF),
        S((n, FF), BF),
        S((n, FF), F32),
    ]
    factor_rows = EXACT_ROWS + -(-FACTOR_BLOCKS * images // 8) * 8
    where = jnp.stack(where_one + top_where).astype(jnp.int32)
    weight_rows = shard_one.shape[0] - rows
    x0, *saved0, x1, gains0, wt0, dn0, flat = pl.pallas_call(
        functools.partial(
            start_kernel, devices, share, images, column_width, row_width, len(pieces_one), None
        ),
        out_shape=[S((n, D), F32)]
        + saved
        + [
            S((n, D), F32),
            S((8, D), F32),
            S((1, WIDE, D), BF),
            S((1, FF, D), BF),
            S((flat_rows, 128), F32),
        ],
        in_specs=[smem] * 2 + [vmem] * (2 * len(pieces_one) + 1),
        out_specs=[vmem] * 13,
        scratch_shapes=[
            pltpu.VMEM((devices, rows, 128), F32),
            pltpu.VMEM((devices, weight_rows, 128), BF),
            pltpu.VMEM((ROWS_OUT, D), F32),
            pltpu.VMEM((4, rows + 8, 128), F32),
            pltpu.VMEM((2, PATCH_DIM, 128), F32),
            pltpu.VMEM((2, TQ, 128), F32),
        ],
        compiler_params=params,
        cost_estimate=cost(20),
        name="start",
    )(info, where, *pieces_one, *top_arrays, patches)

    two, x1 = lax.optimization_barrier((two, x1))
    pieces_two = gather_stages(two, stages[:1], devices)
    *saved1, gains1, gstream, kv, factors, small, wt12, dn12 = pl.pallas_call(
        functools.partial(
            forward_kernel,
            float(images * devices),
            images,
            column_width,
            row_width,
            len(pieces_two),
        ),
        out_shape=saved
        + [
            S((8, D), F32),
            S((n, D), F32),
            S((3 * D, 128), F32),
            S((factor_rows, 128), F32),
            S((16, CLASSES_PAD), F32),
            S((2, WIDE, D), BF),
            S((2, FF, D), BF),
        ],
        in_specs=[smem] * 2 + [vmem] * (len(pieces_two) + 2),
        out_specs=[vmem] * 14,
        scratch_shapes=[
            pltpu.VMEM((devices, shard_two.shape[0], 128), BF),
            pltpu.VMEM((ROWS_OUT, D), F32),
            pltpu.VMEM((8, D, 128), F32),
            pltpu.VMEM((n, D), F32),
            pltpu.VMEM((images, TK, D), BF),
            pltpu.VMEM((images, TK, D), BF),
            pltpu.VMEM((n, D), BF),
            pltpu.VMEM((n, D), BF),
        ]
        + [pltpu.VMEM((16, D), F32)] * 6
        + [pltpu.VMEM((n, D), BF)],
        compiler_params=params,
        cost_estimate=cost(30),
        name="forward",
    )(info, where, flat, x1, *pieces_two)

    mom_shard = jnp.concatenate([jnp.transpose(wide_mom, (0, 2, 1)), down_mom], 1)
    mom_shard, _ = lax.optimization_barrier((mom_shard, pieces_one[:4]))
    mom_all = lax.all_gather(mom_shard, AXES, axis=0)
    factors, mom_all = lax.optimization_barrier((factors, mom_all))
    gstream, factors = lax.optimization_barrier((gstream, factors))
    factors_all = lax.all_gather(factors, AXES, axis=0)
    back_scratch = [
        pltpu.VMEM((n, D), BF),
        pltpu.VMEM((n, FF), BF),
        pltpu.VMEM((n, D), BF),
        pltpu.VMEM((n, D), BF),
        pltpu.VMEM((n, D), BF),
        pltpu.VMEM((n, D), BF),
        pltpu.VMEM((n, D), BF),
        pltpu.VMEM((n, D), BF),
    ]
    gstream1, middle_keep, middle_send, vec1, upb1 = pl.pallas_call(
        functools.partial(middle_kernel, images),
        out_shape=[
            S((n, D), F32),
            S((MIDDLE_ROWS // 2, 128), F32),
            S((MIDDLE_ROWS // 2, 128), F32),
            S((8, D), F32),
            S((8, FF), F32),
        ],
        in_specs=[smem] + [vmem] * 13,
        out_specs=[vmem] * 5,
        scratch_shapes=[pltpu.VMEM((MIDDLE_ROWS, 128), F32)] + back_scratch,
        compiler_params=params,
        cost_estimate=cost(23),
        name="middle",
    )(info, x1, *saved1, gains1, gstream, wt12, dn12, kv)

    first_keep, first_send = pl.pallas_call(
        functools.partial(first_kernel, images),
        out_shape=[S((FIRST_ROWS // 2, 128), F32)] * 2,
        in_specs=[smem] + [vmem] * 16,
        out_specs=[vmem] * 2,
        scratch_shapes=[
            pltpu.VMEM((FIRST_ROWS, 128), F32),
            pltpu.VMEM((n, D), F32),
            pltpu.VMEM((8, D), F32),
            pltpu.VMEM((8, FF), F32),
            pltpu.VMEM((2, PATCH_DIM, 128), F32),
            pltpu.VMEM((2, TQ + 16, 128), F32),
        ]
        + back_scratch,
        compiler_params=params,
        cost_estimate=cost(25),
        name="first",
    )(info, x0, *saved0, gains0, gstream1, wt0, dn0, patches, small, vec1, upb1)

    exact, extra = pl.pallas_call(
        functools.partial(coefficient_kernel, devices),
        grid=(1,),
        out_shape=[S((EXACT_ROWS, 128), F32), S((16, 128), F32)],
        in_specs=[pl.BlockSpec((devices, EXACT_ROWS, 128), lambda i: (0, 0, 0)), vmem],
        out_specs=[vmem] * 2,
        compiler_params=params,
        cost_estimate=cost(2),
        name="coefficients",
    )(factors_all, basis_block)

    g2, headflat = pl.pallas_call(
        functools.partial(late_kernel, devices, images),
        out_shape=[S((ROWS_OUT, D), F32), S((HEAD_ROWS + 4, 128), F32)],
        in_specs=[vmem],
        out_specs=[vmem] * 2,
        scratch_shapes=[pltpu.VMEM((8, D, 128), F32)],
        compiler_params=params,
        cost_estimate=cost(4),
        name="late",
    )(factors_all.reshape(devices * factor_rows, 128))

    split_bits = 5
    for bit in range(split_bits, bits):
        extra = extra + swap(extra, 1 << bit, devices)
    if bits > split_bits:
        c = extra[0] + extra[1] + extra[2]
        split = []
        for k in range(3):
            split.append(lax.reduce_precision(c, 8, 7))
            c = c - split[-1]
        extra = jnp.concatenate([jnp.stack(split), extra[3:]], 0)
    kept = None
    for low, width in number_of:
        ways = 1 << width
        mine = (me >> low) & (ways - 1)
        if kept is None:
            kept = [
                middle_keep + swap(middle_send, 1, devices),
                first_keep + swap(first_send, 1, devices),
            ]
            kept = jnp.concatenate([x.reshape(4, x.shape[0] // 4, 128) for x in kept], 1)
            continue
        total = lax.dynamic_index_in_dim(kept, mine, 0, keepdims=False)
        for m in range(1, ways):
            send = lax.dynamic_index_in_dim(kept, mine ^ m, 0, keepdims=False).astype(BF)
            total = total + swap(send, m << low, devices).astype(F32)
        if low == 1:
            mr = MIDDLE_ROWS // 8
            kept = jnp.concatenate(
                [
                    total[:mr].reshape(4, mr // 4, 128),
                    total[mr:].reshape(4, (total.shape[0] - mr) // 4, 128),
                ],
                1,
            )
        else:
            kept = total
    for bit in range(split_bits, bits):
        small_part = kept.astype(BF)
        kept = small_part.astype(F32) + swap(small_part, 1 << bit, devices).astype(F32)
    piece = jnp.concatenate([kept, extra], 0).astype(BF)[None]
    pieces = gather_stages([piece], number_of, devices)

    first_column = me * column_width
    in_q = first_column < 3 * D
    in_o = first_column < 4 * D
    start = jnp.where(in_q, 0, jnp.where(in_o, 3 * D, 4 * D))
    count = jnp.where(in_q, 3 * D, jnp.where(in_o, D, FF))
    number = ((me & 1) << 4) | (((me >> 1) & 3) << 2) | ((me >> 3) & 3)
    at = me * share
    spots = jnp.stack(
        [start, count, first_column, WIDE + me * row_width, number, at // 128, at % 128]
    )
    wide_shape = (LAYERS, column_width, D)
    down_shape = (LAYERS, row_width, D)
    flat_rows = -(-((devices - 1) * share // 128 + rows + 24) // 8) * 8
    (
        wide_new,
        wide_mom_new,
        wide_copy,
        down_new,
        down_mom_new,
        down_copy,
        share_grad,
        scal,
    ) = pl.pallas_call(
        functools.partial(muon_kernel, column_width, row_width, len(pieces)),
        out_shape=[
            S(wide_shape, F32),
            S(wide_shape, F32),
            S(wide_shape, BF),
            S(down_shape, F32),
            S(down_shape, F32),
            S(down_shape, BF),
            S((rows, 128), F32),
            S((8, 128), F32),
        ],
        in_specs=[smem] + [vmem] * (len(pieces) + 9),
        out_specs=[vmem] * 8,
        scratch_shapes=[
            pltpu.VMEM((flat_rows, 128), F32),
            pltpu.VMEM((MIDDLE_ROWS, 128), BF),
            pltpu.VMEM((FIRST_ROWS, 128), BF),
            pltpu.VMEM((16 * 32, 128), F32),
            pltpu.VMEM((LAYERS, ROWS_OUT + 16, D), F32),
            pltpu.VMEM((2 * LAYERS, D, D), F32),
            pltpu.VMEM((2 * LAYERS, D, D), F32),
        ],
        compiler_params=params,
        cost_estimate=cost(20),
        name="muon",
    )(
        spots.astype(jnp.int32),
        *pieces,
        g2,
        headflat,
        exact,
        basis_block,
        mom_all,
        wide_t,
        jnp.transpose(wide_mom, (0, 2, 1)),
        down_w,
        down_mom,
    )
    grad_norm, _, removed_norm, loss_sum = [scal[k, 0] for k in range(4)]
    clipped = share_grad.reshape(-1)[:share]
    first_new = BETA_ONE * plain_first + (1.0 - BETA_ONE) * clipped
    second_new = BETA_TWO * plain_second + (1.0 - BETA_TWO) * clipped * clipped
    first_hat = first_new / (1.0 - BETA_ONE**STEP)
    second_hat = second_new / (1.0 - BETA_TWO**STEP)
    plain_new = plain - ADAM_RATE * (
        first_hat / (jnp.sqrt(second_hat) + ADAM_EPS) + DECAY_RATE * plain
    )
    plain_copy = plain_new.astype(BF)
    return (
        loss_sum,
        removed_norm,
        grad_norm,
        *[jnp.transpose(x, (0, 2, 1)) for x in (wide_new, wide_mom_new, wide_copy)],
        down_new,
        down_mom_new,
        down_copy,
        plain_new,
        first_new,
        second_new,
        plain_copy,
    )


def solution(mesh):
    placed = (
        P(AXES, None, None),
        P(AXES),
        P(AXES),
        P(None, None, AXES),
        P(None, AXES, None),
        P(AXES),
        P(None, None, AXES),
        P(None, AXES, None),
        P(AXES),
        P(AXES),
        P(None, AXES),
    )
    return jax.shard_map(
        local,
        mesh=mesh,
        in_specs=placed,
        out_specs=(
            P(),
            P(),
            P(),
            P(None, None, AXES),
            P(None, None, AXES),
            P(None, None, AXES),
            P(None, AXES, None),
            P(None, AXES, None),
            P(None, AXES, None),
            P(AXES),
            P(AXES),
            P(AXES),
            P(AXES),
        ),
        check_vma=False,
    )
```

time: 2120 us -> 269 us (0.13)
  blocking collectives: 576 us -> 0 us
  waiting for transfers between devices: 579 us -> 59.5 us
  local copies, waits for them, and re-layouts: 425 us -> 9.31 us
  matrix products: 335 us -> 0 us
  Pallas kernels: 0 us -> 128 us
  other arithmetic: 133 us -> 10.9 us
  starting transfers between devices: 0.56 us -> 42.5 us
  loops' own time: 31 us -> 0 us
    all_gather x12 -> x0, blocking collectives: 496 us -> none  [the longest x3 132 us: backward_step(): lax.all_gather(wide_layer, ('dp', 'fsdp'), axis=1, tiled=True)]
    dot_general x247 -> x0, matrix products: 298 us -> none  [the longest x20 51.9 us: product(): jnp.einsum('ri,ij->rj', left, right, preferred_element_type=jnp.float32)]
    unnamed x6 -> x2, waiting for transfers between devices: 262 us -> 0.03 us
    while x9 -> x0, waiting for transfers between devices: 255 us -> none
    pallas_call x0 -> x7, Pallas kernels: none -> 128 us  [the longest x1 31 us: local(): pl.pallas_call(functools.partial(forward_kernel, float(images * devices),...]
    reduce_sum x62 -> x0, other arithmetic: 91.7 us -> none  [the longest x12 21.4 us: normalize(): return centered * lax.rsqrt(variance + NORM_EPS) * gain + shift]
    reshape x35 -> x0, local copies, waits for them, and re-layouts: 86 us -> none  [the longest x6 14.2 us: layer_parts(): normalize(middle, second_gain, second_shift).astype(jnp.bfloat16)]
    psum x2 -> x0, blocking collectives: 79.8 us -> none  [local(): coefficients, loss_sum = lax.psum((coef_part, loss_local), ('dp', 'fsdp'))]
  transfers between devices with their start and end apart: 10 -> 50, of which waited for: 7 -> 22; matrix products, arithmetic and copies ran while one was open for 17% -> 4% of each run, Pallas kernels for 0% -> 40%
where the time goes in v1:
time: 269 us; the launch traced here: 265 us
  Pallas kernels  128 us (48%)
  waiting for transfers between devices  59.5 us (22%)
  starting transfers between devices  42.5 us (16%)
  between operations  15.1 us (6%)
  other arithmetic  10.9 us (4%)
  local copies, waits for them, and re-layouts  9.31 us (3%)
    ppermute x45, waiting for transfers between devices, swap(): return lax.ppermute(x, AXES, [(i, i ^ mask) for i in range(devices)])  53.2 us
    ppermute x45, starting transfers between devices, swap(): return lax.ppermute(x, AXES, [(i, i ^ mask) for i in range(devices)])  39.8 us
    pallas_call x1, Pallas kernels, local(): pl.pallas_call(functools.partial(forward_kernel, float(images * devices),...  31 us
    pallas_call x1, Pallas kernels, local(): pl.pallas_call(functools.partial(first_kernel, images), out_shape=[S((FIR...  25.6 us
    pallas_call x1, Pallas kernels, local(): pl.pallas_call(functools.partial(middle_kernel, images), out_shape=[S((n,...  23 us
    pallas_call x1, Pallas kernels, local(): pl.pallas_call(functools.partial(start_kernel, devices, share, images, co...  21.3 us
    pallas_call x1, Pallas kernels, local(): pl.pallas_call(functools.partial(muon_kernel, column_width, row_width, le...  20.9 us
    ppermute x3, waiting for transfers between devices, local(): lax.ppermute(low_half, AXES, [(i, i ^ m << 3) for i in range(top, devices)])  6.24 us
  transfers between devices with their start and end apart: 50, of which 22 were waited for; matrix products, arithmetic and copies ran while one was open for 4% of the time, Pallas kernels for 40%

profile of v1, /device:TPU:0, one launch (start us, length us, event | category | flops | bytes accessed | tf_op | source)
XLA Modules:
  0.0 265.1 jit_solution(14516201148201655687)
XLA Ops:
  10.3 3.0 %collective-permute-start = (bf16[1,224,128]{2,1,0:T(8,128)(2,1)S(1)}, bf16[1,224,128]{2,1,0:T(8,128)(2,1)S(1)}, u32[]{:S(2)}, u32[]{:S(2)}) collective-permute-start(bf16[1,224,128]{2,1,0:T(8,128)(2,1)S(1)} %maximum_bitcast_fusion), channel_id=1, source_target_pairs={{0,8},{1,9},{2,10},{3,11},{4,12},{5,13},{6,14},{7,15},{8,0},{9,1},... | collective-permute-start | bytes 172040 | tf_op jit(solution)/shard_map/ppermute | solution.py:1077
  13.3 2.6 collective-permute-start.1
  17.1 3.5 %collective-permute-start.7 = (bf16[1,224,128]{2,1,0:T(8,128)(2,1)S(1)}, bf16[1,224,128]{2,1,0:T(8,128)(2,1)S(1)}, u32[]{:S(2)}, u32[]{:S(2)}) collective-permute-start(bf16[1,224,128]{2,1,0:T(8,128)(2,1)S(1)} %maximum_bitcast_fusion.1), channel_id=1, source_target_pairs={{0,16},{1,17},{2,18},{3,19},{4,20},{5,21},{6,22},{7,23},{8,24},{9,... | collective-permute-start | bytes 172040 | tf_op jit(solution)/shard_map/ppermute | solution.py:1077
  20.6 1.5 collective-permute-done.2
  22.1 1.6 collective-permute-start.3
  23.7 1.5 collective-permute-start.4
  26.6 3.6 %collective-permute-done.3.refs_1_ = bf16[4,224,128]{2,1,0:T(8,128)(2,1)S(1)} collective-permute-done((bf16[4,224,128]{2,1,0:T(8,128)(2,1)S(1)}, bf16[4,224,128]{2,1,0:T(8,128)(2,1)S(1)}, u32[]{:S(2)}, u32[]{:S(2)}) %collective-permute-start.3) | collective-permute-done | bytes 229408 | tf_op jit(solution)/shard_map/ppermute | solution.py:1077
  30.2 3.6 %collective-permute-done.4.refs_2_ = bf16[4,224,128]{2,1,0:T(8,128)(2,1)S(1)} collective-permute-done((bf16[4,224,128]{2,1,0:T(8,128)(2,1)S(1)}, bf16[4,224,128]{2,1,0:T(8,128)(2,1)S(1)}, u32[]{:S(2)}, u32[]{:S(2)}) %collective-permute-start.4) | collective-permute-done | bytes 229408 | tf_op jit(solution)/shard_map/ppermute | solution.py:1077
  35.3 1.3 collective-permute-start.18
  36.6 6.2 %collective-permute-done.18 = bf16[112,128]{1,0:T(8,128)(2,1)S(1)} collective-permute-done((bf16[112,128]{1,0:T(8,128)(2,1)S(1)}, bf16[112,128]{1,0:T(8,128)(2,1)S(1)}, u32[]{:S(2)}, u32[]{:S(2)}) %collective-permute-start.18) | collective-permute-done | bytes 28704 | tf_op jit(solution)/shard_map/ppermute | solution.py:1121
  42.9 1.3 collective-permute-start.19
  45.0 1.4 collective-permute-start.21
  47.0 1.0 collective-permute-done.20.refs_10_
  48.0 1.7 collective-permute-done.21.refs_11_
  49.8 1.2 collective-permute-done.22.refs_12_
  51.1 1.0 collective-permute-done.23.refs_13_
  52.3 1.2 collective-permute-done.24.refs_14_
  54.3 1.6 copy.26.refs_16_.refs_12_
  56.7 1.2 collective-permute-start.10
  57.9 1.8 collective-permute-start.11
  60.2 21.3 %start.1 = (f32[1344,192]{1,0:T(8,128)}, f32[1344,192]{1,0:T(8,128)}, bf16[1344,192]{1,0:T(8,128)(2,1)}, bf16[4,384,192]{2,1,0:T(8,128)(2,1)}, bf16[4,384,192]{2...) custom-call(s32[9]{0:T(128)} %pad_add_fusion.info, ...), custom_call_target="tpu_custom_call" | custom-call | flops 23000000512 | bytes 20000000 | tf_op jit(solution)/shard_map/start/pallas_call | solution.py:1158
  84.9 31.0 %forward.1 = (f32[1344,192]{1,0:T(8,128)}, bf16[1344,192]{1,0:T(8,128)(2,1)}, bf16[4,384,192]{2,1,0:T(8,128)(2,1)}, bf16[4,384,192]{2,1,0:T(8,128)(2,1)}, bf16[1...) custom-call(s32[9]{0:T(128)} %pad_add_fusion.info, ...), custom_call_target="tpu_custom_call" | custom-call | flops 34500001792 | bytes 30000000 | tf_op jit(solution)/shard_map/forward/pallas_call | solution.py:1188
  115.9 23.0 %middle.1 = (f32[1344,192]{1,0:T(8,128)}, f32[2048,128]{1,0:T(8,128)}, f32[2048,128]{1,0:T(8,128)}, f32[8,192]{1,0:T(8,128)}, f32[8,768]{1,0:T(8,128)}) custom-call(s32[9]{0:T(128)} %pad_add_fusion.info, f32[1344,192]{1,0:T(8,128)} %get-tuple-element.80.x1.refs_0_, f32[1344,192]{1,0:T(8,128)} %get-tuple-element.86.refs_1_, ...), custom_call_target="tpu_custom_call" | custom-call | flops 26449999872 | bytes 23000000 | tf_op jit(solution)/shard_map/middle/pallas_call | solution.py:1242
  138.9 25.6 %first.1 = (f32[2816,128]{1,0:T(8,128)}, f32[2816,128]{1,0:T(8,128)}) custom-call(s32[9]{0:T(128)} %pad_add_fusion.info, f32[1344,192]{1,0:T(8,128)} %get-tuple-element.104.refs_0_, f32[1344,192]{1,0:T(8,128)} %get-tuple-element.105.refs_1_, bf16[1344,192]{1,0:T(8,128)(2,1)} %get-tuple-element.106.refs_2_, bf16[4,384,192]{2,1,0:T(8,128)(2,1)} %get-tuple-element.107.refs_3_, ...), custom_call_target="tpu_custom_call" | custom-call | flops 28750000128 | bytes 25000000 | tf_op jit(solution)/shard_map/first/pallas_call | solution.py:1259
  165.0 5.0 %collective-permute-done.30 = f32[2048,128]{1,0:T(8,128)S(1)} collective-permute-done((f32[2048,128]{1,0:T(8,128)}, f32[2048,128]{1,0:T(8,128)S(1)}, u32[]{:S(2)}, u32[]{:S(2)}) %collective-permute-start.30) | collective-permute-done | bytes 1048608 | tf_op jit(solution)/shard_map/ppermute | solution.py:1077
  171.0 1.4 add.95
  172.5 1.1 copy-done.3
  173.6 1.6 add.96
  175.1 1.1 fusion.12
  176.2 1.8 collective-permute-start.32
  179.7 6.9 %collective-permute-done.32 = bf16[1216,128]{1,0:T(8,128)(2,1)S(1)} collective-permute-done((bf16[1216,128]{1,0:T(8,128)(2,1)}, bf16[1216,128]{1,0:T(8,128)(2,1)S(1)}, u32[]{:S(2)}, u32[]{:S(2)}) %collective-permute-start.32) | collective-permute-done | bytes 311328 | tf_op jit(solution)/shard_map/ppermute | solution.py:1077
  186.6 7.3 %collective-permute-done.33 = bf16[1216,128]{1,0:T(8,128)(2,1)S(1)} collective-permute-done((bf16[1216,128]{1,0:T(8,128)(2,1)}, bf16[1216,128]{1,0:T(8,128)(2,1)S(1)}, u32[]{:S(2)}, u32[]{:S(2)}) %collective-permute-start.33) | collective-permute-done | bytes 311328 | tf_op jit(solution)/shard_map/ppermute | solution.py:1077
  194.4 4.3 %collective-permute-start.37 = (bf16[304,128]{1,0:T(8,128)(2,1)S(1)}, bf16[304,128]{1,0:T(8,128)(2,1)S(1)}, u32[]{:S(2)}, u32[]{:S(2)}) collective-permute-start(bf16[304,128]{1,0:T(8,128)(2,1)S(1)} %get-tuple-element.143), channel_id=1, source_target_pairs={{0,24},{1,25},{2,26},{3,27},{4,28},{5,29},{6,30},{7,31},{8,16},{9,... | collective-permute-start | bytes 233480 | tf_op jit(solution)/shard_map/ppermute | solution.py:1077
  199.6 3.2 %collective-permute-done.36 = bf16[304,128]{1,0:T(8,128)(2,1)S(1)} collective-permute-done((bf16[304,128]{1,0:T(8,128)(2,1)S(1)}, bf16[304,128]{1,0:T(8,128)(2,1)S(1)}, u32[]{:S(2)}, u32[]{:S(2)}) %collective-permute-start.36) | collective-permute-done | bytes 77856 | tf_op jit(solution)/shard_map/ppermute | solution.py:1077
  202.9 2.0 coefficients.1
  205.6 1.5 collective-permute-start.38
  207.1 1.4 collective-permute-start.39
  208.4 1.6 collective-permute-start.40
  210.1 1.8 collective-permute-done.38
  211.8 3.0 %collective-permute-done.39 = bf16[1,320,128]{2,1,0:T(8,128)(2,1)S(1)} collective-permute-done((bf16[1,320,128]{2,1,0:T(8,128)(2,1)S(1)}, bf16[1,320,128]{2,1,0:T(8,128)(2,1)S(1)}, u32[]{:S(2)}, u32[]{:S(2)}) %collective-permute-start.39) | collective-permute-done | bytes 81952 | tf_op jit(solution)/shard_map/ppermute | solution.py:1077
  215.8 1.1 collective-permute-start.42
  216.9 1.5 collective-permute-start.43
  219.1 5.4 %collective-permute-done.41.refs_1_ = bf16[4,320,128]{2,1,0:T(8,128)(2,1)S(1)} collective-permute-done((bf16[4,320,128]{2,1,0:T(8,128)(2,1)S(1)}, bf16[4,320,128]{2,1,0:T(8,128)(2,1)S(1)}, u32[]{:S(2)}, u32[]{:S(2)}) %collective-permute-start.41) | collective-permute-done | bytes 327712 | tf_op jit(solution)/shard_map/ppermute | solution.py:1077
  224.5 4.0 %collective-permute-done.42.refs_2_ = bf16[4,320,128]{2,1,0:T(8,128)(2,1)S(1)} collective-permute-done((bf16[4,320,128]{2,1,0:T(8,128)(2,1)S(1)}, bf16[4,320,128]{2,1,0:T(8,128)(2,1)S(1)}, u32[]{:S(2)}, u32[]{:S(2)}) %collective-permute-start.42) | collective-permute-done | bytes 327712 | tf_op jit(solution)/shard_map/ppermute | solution.py:1077
  229.0 3.9 %late.1 = (f32[2304,192]{1,0:T(8,128)}, f32[1504,128]{1,0:T(8,128)}) custom-call(f32[4864,128]{1,0:T(8,128)} %all-gather.7.cloned.1.call-done.gathered), custom_call_target="tpu_custom_call" | custom-call | flops 4600000000 | bytes 4000000 | tf_op jit(solution)/shard_map/late/pallas_call | solution.py:1289
  234.1 20.9 %muon.1 = (f32[3,48,192]{2,1,0:T(8,128)}, f32[3,48,192]{2,1,0:T(8,128)}, bf16[3,48,192]{2,1,0:T(8,128)(2,1)}, f32[3,24,192]{2,1,0:T(8,128)}, f32[3,24,192]{2,1,0...) custom-call(s32[7]{0:T(128)} %stack.154.place, bf16[4,320,128]{2,1,0:T(8,128)(2,1)} %copy-done.6, ...), custom_call_target="tpu_custom_call" | custom-call | flops 23000000512 | bytes 20000000 | tf_op jit(solution)/shard_map/muon/pallas_call | solution.py:1364
  255.0 1.3 fusion.35
  256.3 1.5 fusion.32
  (182 shorter events, 22.5 us)
Async XLA Ops:
  7.2 108.7 %all-gather.5.cloned.1.call-start = ((), (), s32[]{:S(2)}) async-start(), calls=%async_computation | async-start | bytes 7299072 | tf_op jit(solution)/shard_map/all_gather | solution.py:1228
  10.3 10.3 %collective-permute-start = (bf16[1,224,128]{2,1,0:T(8,128)(2,1)S(1)}, bf16[1,224,128]{2,1,0:T(8,128)(2,1)S(1)}, u32[]{:S(2)}, u32[]{:S(2)}) collective-permute-start(bf16[1,224,128]{2,1,0:T(8,128)(2,1)S(1)} %maximum_bitcast_fusion), channel_id=1, source_target_pairs={{0,8},{1,9},{2,10},{3,11},{4,12},{5,13},{6,14},{7,15},{8,0},{9,1},... | collective-permute-start | bytes 172040 | tf_op jit(solution)/shard_map/ppermute | solution.py:1077
  13.3 7.3 %collective-permute-start.1 = (bf16[1,224,128]{2,1,0:T(8,128)(2,1)S(1)}, bf16[1,224,128]{2,1,0:T(8,128)(2,1)S(1)}, u32[]{:S(2)}, u32[]{:S(2)}) collective-permute-start(bf16[1,224,128]{2,1,0:T(8,128)(2,1)S(1)} %maximum_bitcast_fusion), channel_id=1, source_target_pairs={{0,16},{1,17},{2,18},{3,19},{4,20},{5,21},{6,22},{7,23},{8,24},{9,... | collective-permute-start | bytes 172040 | tf_op jit(solution)/shard_map/ppermute | solution.py:1077
  15.9 6.2 %collective-permute-start.2 = (bf16[1,224,128]{2,1,0:T(8,128)(2,1)S(1)}, bf16[1,224,128]{2,1,0:T(8,128)(2,1)S(1)}, u32[]{:S(2)}, u32[]{:S(2)}) collective-permute-start(bf16[1,224,128]{2,1,0:T(8,128)(2,1)S(1)} %maximum_bitcast_fusion), channel_id=1, source_target_pairs={{0,24},{1,25},{2,26},{3,27},{4,28},{5,29},{6,30},{7,31},{8,16},{9,... | collective-permute-start | bytes 172040 | tf_op jit(solution)/shard_map/ppermute | solution.py:1077
  16.1 9.1 %collective-permute-start.6 = (bf16[1,224,128]{2,1,0:T(8,128)(2,1)S(1)}, bf16[1,224,128]{2,1,0:T(8,128)(2,1)S(1)}, u32[]{:S(2)}, u32[]{:S(2)}) collective-permute-start(bf16[1,224,128]{2,1,0:T(8,128)(2,1)S(1)} %maximum_bitcast_fusion.1), channel_id=1, source_target_pairs={{0,8},{1,9},{2,10},{3,11},{4,12},{5,13},{6,14},{7,15},{8,0},{9,1},... | collective-permute-start | bytes 172040 | tf_op jit(solution)/shard_map/ppermute | solution.py:1077
  17.1 9.3 %collective-permute-start.7 = (bf16[1,224,128]{2,1,0:T(8,128)(2,1)S(1)}, bf16[1,224,128]{2,1,0:T(8,128)(2,1)S(1)}, u32[]{:S(2)}, u32[]{:S(2)}) collective-permute-start(bf16[1,224,128]{2,1,0:T(8,128)(2,1)S(1)} %maximum_bitcast_fusion.1), channel_id=1, source_target_pairs={{0,16},{1,17},{2,18},{3,19},{4,20},{5,21},{6,22},{7,23},{8,24},{9,... | collective-permute-start | bytes 172040 | tf_op jit(solution)/shard_map/ppermute | solution.py:1077
  20.6 6.0 %collective-permute-start.8 = (bf16[1,224,128]{2,1,0:T(8,128)(2,1)S(1)}, bf16[1,224,128]{2,1,0:T(8,128)(2,1)S(1)}, u32[]{:S(2)}, u32[]{:S(2)}) collective-permute-start(bf16[1,224,128]{2,1,0:T(8,128)(2,1)S(1)} %maximum_bitcast_fusion.1), channel_id=1, source_target_pairs={{0,24},{1,25},{2,26},{3,27},{4,28},{5,29},{6,30},{7,31},{8,16},{9,... | collective-permute-start | bytes 172040 | tf_op jit(solution)/shard_map/ppermute | solution.py:1077
  22.1 8.1 %collective-permute-start.3 = (bf16[4,224,128]{2,1,0:T(8,128)(2,1)S(1)}, bf16[4,224,128]{2,1,0:T(8,128)(2,1)S(1)}, u32[]{:S(2)}, u32[]{:S(2)}) collective-permute-start(bf16[4,224,128]{2,1,0:T(8,128)(2,1)S(1)} %pad_maximum_fusion.1.refs_0_), channel_id=1, source_target_pairs={{0,2},{1,3},{2,0},{3,1},{4,6},{5,7},{6,4},{7,5},{8,10},{9,11},{10,... | collective-permute-start | bytes 688136 | tf_op jit(solution)/shard_map/ppermute | solution.py:1077
  23.7 10.1 %collective-permute-start.4 = (bf16[4,224,128]{2,1,0:T(8,128)(2,1)S(1)}, bf16[4,224,128]{2,1,0:T(8,128)(2,1)S(1)}, u32[]{:S(2)}, u32[]{:S(2)}) collective-permute-start(bf16[4,224,128]{2,1,0:T(8,128)(2,1)S(1)} %pad_maximum_fusion.1.refs_0_), channel_id=1, source_target_pairs={{0,4},{1,5},{2,6},{3,7},{4,0},{5,1},{6,2},{7,3},{8,12},{9,13},{10,... | collective-permute-start | bytes 688136 | tf_op jit(solution)/shard_map/ppermute | solution.py:1077
  25.2 8.6 %collective-permute-start.5 = (bf16[4,224,128]{2,1,0:T(8,128)(2,1)S(1)}, bf16[4,224,128]{2,1,0:T(8,128)(2,1)S(1)}, u32[]{:S(2)}, u32[]{:S(2)}) collective-permute-start(bf16[4,224,128]{2,1,0:T(8,128)(2,1)S(1)} %pad_maximum_fusion.1.refs_0_), channel_id=1, source_target_pairs={{0,6},{1,7},{2,4},{3,5},{4,2},{5,3},{6,0},{7,1},{8,14},{9,15},{10,... | collective-permute-start | bytes 688136 | tf_op jit(solution)/shard_map/ppermute | solution.py:1077
  33.9 169.0 %all-gather.7.cloned.1.call-start = ((), (), s32[]{:S(2)}) async-start(), calls=%async_computation.1 | async-start | bytes 2568192 | tf_op jit(solution)/shard_map/all_gather | solution.py:1231
  33.9 2.7 %collective-permute-start.16 = (bf16[112,128]{1,0:T(8,128)(2,1)S(1)}, bf16[112,128]{1,0:T(8,128)(2,1)S(1)}, u32[]{:S(2)}, u32[]{:S(2)}) collective-permute-start(bf16[112,128]{1,0:T(8,128)(2,1)S(1)} %get-tuple-element.147), channel_id=1, source_target_pairs={{24,16},{25,17},{26,18},{27,19},{28,20},{29,21},{30,22},{31,23}} | collective-permute-start | bytes 86024 | tf_op jit(solution)/shard_map/ppermute | solution.py:1121
  34.6 2.0 collective-permute-start.17
  35.3 7.6 %collective-permute-start.18 = (bf16[112,128]{1,0:T(8,128)(2,1)S(1)}, bf16[112,128]{1,0:T(8,128)(2,1)S(1)}, u32[]{:S(2)}, u32[]{:S(2)}) collective-permute-start(bf16[112,128]{1,0:T(8,128)(2,1)S(1)} %get-tuple-element.147), channel_id=1, source_target_pairs={{24,0},{25,1},{26,2},{27,3},{28,4},{29,5},{30,6},{31,7}} | collective-permute-start | bytes 86024 | tf_op jit(solution)/shard_map/ppermute | solution.py:1121
  42.9 4.1 %collective-permute-start.19 = (bf16[1,112,128]{2,1,0:T(8,128)(2,1)S(1)}, bf16[1,112,128]{2,1,0:T(8,128)(2,1)S(1)}, u32[]{:S(2)}, u32[]{:S(2)}) collective-permute-start(bf16[1,112,128]{2,1,0:T(8,128)(2,1)S(1)} %select_bitcast_fusion.refs_8_), channel_id=1, source_target_pairs={{0,2},{1,3},{2,0},{3,1},{4,6},{5,7},{6,4},{7,5},{8,10},{9,11},{10,... | collective-permute-start | bytes 86024 | tf_op jit(solution)/shard_map/ppermute | solution.py:1077
  44.2 3.9 %collective-permute-start.20 = (bf16[1,112,128]{2,1,0:T(8,128)(2,1)S(1)}, bf16[1,112,128]{2,1,0:T(8,128)(2,1)S(1)}, u32[]{:S(2)}, u32[]{:S(2)}) collective-permute-start(bf16[1,112,128]{2,1,0:T(8,128)(2,1)S(1)} %select_bitcast_fusion.refs_8_), channel_id=1, source_target_pairs={{0,4},{1,5},{2,6},{3,7},{4,0},{5,1},{6,2},{7,3},{8,12},{9,13},{10,... | collective-permute-start | bytes 86024 | tf_op jit(solution)/shard_map/ppermute | solution.py:1077
  45.0 4.8 %collective-permute-start.21 = (bf16[1,112,128]{2,1,0:T(8,128)(2,1)S(1)}, bf16[1,112,128]{2,1,0:T(8,128)(2,1)S(1)}, u32[]{:S(2)}, u32[]{:S(2)}) collective-permute-start(bf16[1,112,128]{2,1,0:T(8,128)(2,1)S(1)} %select_bitcast_fusion.refs_8_), channel_id=1, source_target_pairs={{0,6},{1,7},{2,4},{3,5},{4,2},{5,3},{6,0},{7,1},{8,14},{9,15},{10,... | collective-permute-start | bytes 86024 | tf_op jit(solution)/shard_map/ppermute | solution.py:1077
  46.4 11.5 %collective-permute-start.12 = (bf16[4,224,128]{2,1,0:T(8,128)(2,1)S(1)}, bf16[4,224,128]{2,1,0:T(8,128)(2,1)S(1)}, u32[]{:S(2)}, u32[]{:S(2)}) collective-permute-start(bf16[4,224,128]{2,1,0:T(8,128)(2,1)S(1)} %pad_maximum_fusion.1.refs_0_), channel_id=1, source_target_pairs={{0,1},{1,0},{2,3},{3,2},{4,5},{5,4},{6,7},{7,6},{8,9},{9,8},{10,11... | collective-permute-start | bytes 688136 | tf_op jit(solution)/shard_map/ppermute | solution.py:1077
  46.4 13.2 %collective-permute-start.13 = (bf16[4,224,128]{2,1,0:T(8,128)(2,1)S(1)}, bf16[4,224,128]{2,1,0:T(8,128)(2,1)}, u32[]{:S(2)}, u32[]{:S(2)}) collective-permute-start(bf16[4,224,128]{2,1,0:T(8,128)(2,1)S(1)} %collective-permute-done.3.refs_1_), channel_id=1, source_target_pairs={{0,1},{1,0},{2,3},{3,2},{4,5},{5,4},{6,7},{7,6},{8,9},{9,8},{10,11... | collective-permute-start | bytes 688136 | tf_op jit(solution)/shard_map/ppermute | solution.py:1077
  46.9 13.3 %collective-permute-start.14 = (bf16[4,224,128]{2,1,0:T(8,128)(2,1)S(1)}, bf16[4,224,128]{2,1,0:T(8,128)(2,1)}, u32[]{:S(2)}, u32[]{:S(2)}) collective-permute-start(bf16[4,224,128]{2,1,0:T(8,128)(2,1)S(1)} %collective-permute-done.4.refs_2_), channel_id=1, source_target_pairs={{0,1},{1,0},{2,3},{3,2},{4,5},{5,4},{6,7},{7,6},{8,9},{9,8},{10,11... | collective-permute-start | bytes 688136 | tf_op jit(solution)/shard_map/ppermute | solution.py:1077
  48.0 12.2 %collective-permute-start.15 = (bf16[4,224,128]{2,1,0:T(8,128)(2,1)S(1)}, bf16[4,224,128]{2,1,0:T(8,128)(2,1)}, u32[]{:S(2)}, u32[]{:S(2)}) collective-permute-start(bf16[4,224,128]{2,1,0:T(8,128)(2,1)S(1)} %collective-permute-done.5.refs_3_), channel_id=1, source_target_pairs={{0,1},{1,0},{2,3},{3,2},{4,5},{5,4},{6,7},{7,6},{8,9},{9,8},{10,11... | collective-permute-start | bytes 688136 | tf_op jit(solution)/shard_map/ppermute | solution.py:1077
  52.2 1.3 collective-permute-start.24
  53.5 3.2 %collective-permute-start.25 = (bf16[1,112,128]{2,1,0:T(8,128)(2,1)S(1)}, bf16[1,112,128]{2,1,0:T(8,128)(2,1)}, u32[]{:S(2)}, u32[]{:S(2)}) collective-permute-start(bf16[1,112,128]{2,1,0:T(8,128)(2,1)S(1)} %collective-permute-done.21.refs_11_), channel_id=1, source_target_pairs={{0,1},{1,0},{2,3},{3,2},{4,5},{5,4},{6,7},{7,6},{8,9},{9,8},{10,11... | collective-permute-start | bytes 86024 | tf_op jit(solution)/shard_map/ppermute | solution.py:1077
  56.7 24.9 %collective-permute-start.10 = (bf16[4,224,128]{2,1,0:T(8,128)(2,1)S(1)}, bf16[4,224,128]{2,1,0:T(8,128)(2,1)S(1)}, u32[]{:S(2)}, u32[]{:S(2)}) collective-permute-start(bf16[4,224,128]{2,1,0:T(8,128)(2,1)S(1)} %pad_maximum_fusion.2.refs_0_), channel_id=1, source_target_pairs={{0,4},{1,5},{2,6},{3,7},{4,0},{5,1},{6,2},{7,3},{8,12},{9,13},{10,... | collective-permute-start | bytes 688136 | tf_op jit(solution)/shard_map/ppermute | solution.py:1077
  57.9 23.7 %collective-permute-start.11 = (bf16[4,224,128]{2,1,0:T(8,128)(2,1)S(1)}, bf16[4,224,128]{2,1,0:T(8,128)(2,1)S(1)}, u32[]{:S(2)}, u32[]{:S(2)}) collective-permute-start(bf16[4,224,128]{2,1,0:T(8,128)(2,1)S(1)} %pad_maximum_fusion.2.refs_0_), channel_id=1, source_target_pairs={{0,6},{1,7},{2,4},{3,5},{4,2},{5,3},{6,0},{7,1},{8,14},{9,15},{10,... | collective-permute-start | bytes 688136 | tf_op jit(solution)/shard_map/ppermute | solution.py:1077
  59.7 21.9 %collective-permute-start.9 = (bf16[4,224,128]{2,1,0:T(8,128)(2,1)S(1)}, bf16[4,224,128]{2,1,0:T(8,128)(2,1)S(1)}, u32[]{:S(2)}, u32[]{:S(2)}) collective-permute-start(bf16[4,224,128]{2,1,0:T(8,128)(2,1)S(1)} %pad_maximum_fusion.2.refs_0_), channel_id=1, source_target_pairs={{0,2},{1,3},{2,0},{3,1},{4,6},{5,7},{6,4},{7,5},{8,10},{9,11},{10,... | collective-permute-start | bytes 688136 | tf_op jit(solution)/shard_map/ppermute | solution.py:1077
  81.6 1.6 collective-permute-start.26
  81.7 1.8 collective-permute-start.27
  82.2 1.6 collective-permute-start.28
  82.3 1.9 collective-permute-start.29
  164.5 8.0 %collective-permute-start.31 = (f32[2816,128]{1,0:T(8,128)}, f32[2816,128]{1,0:T(8,128)S(1)}, u32[]{:S(2)}, u32[]{:S(2)}) collective-permute-start(f32[2816,128]{1,0:T(8,128)} %get-tuple-element.120), channel_id=1, source_target_pairs={{0,1},{1,0},{2,3},{3,2},{4,5},{5,4},{6,7},{7,6},{8,9},{9,8},{10,11... | collective-permute-start | bytes 4325384 | tf_op jit(solution)/shard_map/ppermute | solution.py:1077
  164.7 5.3 %collective-permute-start.30 = (f32[2048,128]{1,0:T(8,128)}, f32[2048,128]{1,0:T(8,128)S(1)}, u32[]{:S(2)}, u32[]{:S(2)}) collective-permute-start(f32[2048,128]{1,0:T(8,128)} %get-tuple-element.103), channel_id=1, source_target_pairs={{0,1},{1,0},{2,3},{3,2},{4,5},{5,4},{6,7},{7,6},{8,9},{9,8},{10,11... | collective-permute-start | bytes 3145736 | tf_op jit(solution)/shard_map/ppermute | solution.py:1077
  176.2 10.4 %collective-permute-start.32 = (bf16[1216,128]{1,0:T(8,128)(2,1)}, bf16[1216,128]{1,0:T(8,128)(2,1)S(1)}, u32[]{:S(2)}, u32[]{:S(2)}) collective-permute-start(bf16[1216,128]{1,0:T(8,128)(2,1)} %get-tuple-element.138), channel_id=1, source_target_pairs={{0,2},{1,3},{2,0},{3,1},{4,6},{5,7},{6,4},{7,5},{8,10},{9,11},{10,... | collective-permute-start | bytes 933896 | tf_op jit(solution)/shard_map/ppermute | solution.py:1077
  178.0 16.0 %collective-permute-start.33 = (bf16[1216,128]{1,0:T(8,128)(2,1)}, bf16[1216,128]{1,0:T(8,128)(2,1)S(1)}, u32[]{:S(2)}, u32[]{:S(2)}) collective-permute-start(bf16[1216,128]{1,0:T(8,128)(2,1)} %get-tuple-element.139), channel_id=1, source_target_pairs={{0,4},{1,5},{2,6},{3,7},{4,0},{5,1},{6,2},{7,3},{8,12},{9,13},{10,... | collective-permute-start | bytes 933896 | tf_op jit(solution)/shard_map/ppermute | solution.py:1077
  178.9 15.1 %collective-permute-start.34 = (bf16[1216,128]{1,0:T(8,128)(2,1)}, bf16[1216,128]{1,0:T(8,128)(2,1)S(1)}, u32[]{:S(2)}, u32[]{:S(2)}) collective-permute-start(bf16[1216,128]{1,0:T(8,128)(2,1)} %get-tuple-element.140), channel_id=1, source_target_pairs={{0,6},{1,7},{2,4},{3,5},{4,2},{5,3},{6,0},{7,1},{8,14},{9,15},{10,... | collective-permute-start | bytes 933896 | tf_op jit(solution)/shard_map/ppermute | solution.py:1077
  194.2 5.4 %collective-permute-start.35 = (bf16[304,128]{1,0:T(8,128)(2,1)S(1)}, bf16[304,128]{1,0:T(8,128)(2,1)S(1)}, u32[]{:S(2)}, u32[]{:S(2)}) collective-permute-start(bf16[304,128]{1,0:T(8,128)(2,1)S(1)} %get-tuple-element.141), channel_id=1, source_target_pairs={{0,8},{1,9},{2,10},{3,11},{4,12},{5,13},{6,14},{7,15},{8,0},{9,1},... | collective-permute-start | bytes 233480 | tf_op jit(solution)/shard_map/ppermute | solution.py:1077
  194.3 8.5 %collective-permute-start.36 = (bf16[304,128]{1,0:T(8,128)(2,1)S(1)}, bf16[304,128]{1,0:T(8,128)(2,1)S(1)}, u32[]{:S(2)}, u32[]{:S(2)}) collective-permute-start(bf16[304,128]{1,0:T(8,128)(2,1)S(1)} %get-tuple-element.142), channel_id=1, source_target_pairs={{0,16},{1,17},{2,18},{3,19},{4,20},{5,21},{6,22},{7,23},{8,24},{9,... | collective-permute-start | bytes 233480 | tf_op jit(solution)/shard_map/ppermute | solution.py:1077
  194.4 8.4 %collective-permute-start.37 = (bf16[304,128]{1,0:T(8,128)(2,1)S(1)}, bf16[304,128]{1,0:T(8,128)(2,1)S(1)}, u32[]{:S(2)}, u32[]{:S(2)}) collective-permute-start(bf16[304,128]{1,0:T(8,128)(2,1)S(1)} %get-tuple-element.143), channel_id=1, source_target_pairs={{0,24},{1,25},{2,26},{3,27},{4,28},{5,29},{6,30},{7,31},{8,16},{9,... | collective-permute-start | bytes 233480 | tf_op jit(solution)/shard_map/ppermute | solution.py:1077
  205.6 6.2 %collective-permute-start.38 = (bf16[1,320,128]{2,1,0:T(8,128)(2,1)S(1)}, bf16[1,320,128]{2,1,0:T(8,128)(2,1)S(1)}, u32[]{:S(2)}, u32[]{:S(2)}) collective-permute-start(bf16[1,320,128]{2,1,0:T(8,128)(2,1)S(1)} %pad_maximum_fusion.4), channel_id=1, source_target_pairs={{0,8},{1,9},{2,10},{3,11},{4,12},{5,13},{6,14},{7,15},{8,0},{9,1},... | collective-permute-start | bytes 245768 | tf_op jit(solution)/shard_map/ppermute | solution.py:1077
  207.1 7.7 %collective-permute-start.39 = (bf16[1,320,128]{2,1,0:T(8,128)(2,1)S(1)}, bf16[1,320,128]{2,1,0:T(8,128)(2,1)S(1)}, u32[]{:S(2)}, u32[]{:S(2)}) collective-permute-start(bf16[1,320,128]{2,1,0:T(8,128)(2,1)S(1)} %pad_maximum_fusion.4), channel_id=1, source_target_pairs={{0,16},{1,17},{2,18},{3,19},{4,20},{5,21},{6,22},{7,23},{8,24},{9,... | collective-permute-start | bytes 245768 | tf_op jit(solution)/shard_map/ppermute | solution.py:1077
  208.4 6.4 %collective-permute-start.40 = (bf16[1,320,128]{2,1,0:T(8,128)(2,1)S(1)}, bf16[1,320,128]{2,1,0:T(8,128)(2,1)S(1)}, u32[]{:S(2)}, u32[]{:S(2)}) collective-permute-start(bf16[1,320,128]{2,1,0:T(8,128)(2,1)S(1)} %pad_maximum_fusion.4), channel_id=1, source_target_pairs={{0,24},{1,25},{2,26},{3,27},{4,28},{5,29},{6,30},{7,31},{8,16},{9,... | collective-permute-start | bytes 245768 | tf_op jit(solution)/shard_map/ppermute | solution.py:1077
  214.9 9.6 %collective-permute-start.41 = (bf16[4,320,128]{2,1,0:T(8,128)(2,1)S(1)}, bf16[4,320,128]{2,1,0:T(8,128)(2,1)S(1)}, u32[]{:S(2)}, u32[]{:S(2)}) collective-permute-start(bf16[4,320,128]{2,1,0:T(8,128)(2,1)S(1)} %pad_maximum_fusion.refs_0_), channel_id=1, source_target_pairs={{0,2},{1,3},{2,0},{3,1},{4,6},{5,7},{6,4},{7,5},{8,10},{9,11},{10,... | collective-permute-start | bytes 983048 | tf_op jit(solution)/shard_map/ppermute | solution.py:1077
  215.8 12.7 %collective-permute-start.42 = (bf16[4,320,128]{2,1,0:T(8,128)(2,1)S(1)}, bf16[4,320,128]{2,1,0:T(8,128)(2,1)S(1)}, u32[]{:S(2)}, u32[]{:S(2)}) collective-permute-start(bf16[4,320,128]{2,1,0:T(8,128)(2,1)S(1)} %pad_maximum_fusion.refs_0_), channel_id=1, source_target_pairs={{0,4},{1,5},{2,6},{3,7},{4,0},{5,1},{6,2},{7,3},{8,12},{9,13},{10,... | collective-permute-start | bytes 983048 | tf_op jit(solution)/shard_map/ppermute | solution.py:1077
  216.9 11.6 %collective-permute-start.43 = (bf16[4,320,128]{2,1,0:T(8,128)(2,1)S(1)}, bf16[4,320,128]{2,1,0:T(8,128)(2,1)S(1)}, u32[]{:S(2)}, u32[]{:S(2)}) collective-permute-start(bf16[4,320,128]{2,1,0:T(8,128)(2,1)S(1)} %pad_maximum_fusion.refs_0_), channel_id=1, source_target_pairs={{0,6},{1,7},{2,4},{3,5},{4,2},{5,3},{6,0},{7,1},{8,14},{9,15},{10,... | collective-permute-start | bytes 983048 | tf_op jit(solution)/shard_map/ppermute | solution.py:1077
  219.1 13.9 %collective-permute-start.44 = (bf16[4,320,128]{2,1,0:T(8,128)(2,1)S(1)}, bf16[4,320,128]{2,1,0:T(8,128)(2,1)S(1)}, u32[]{:S(2)}, u32[]{:S(2)}) collective-permute-start(bf16[4,320,128]{2,1,0:T(8,128)(2,1)S(1)} %pad_maximum_fusion.refs_0_), channel_id=1, source_target_pairs={{0,1},{1,0},{2,3},{3,2},{4,5},{5,4},{6,7},{7,6},{8,9},{9,8},{10,11... | collective-permute-start | bytes 983048 | tf_op jit(solution)/shard_map/ppermute | solution.py:1077
  224.5 8.5 %collective-permute-start.45 = (bf16[4,320,128]{2,1,0:T(8,128)(2,1)S(1)}, bf16[4,320,128]{2,1,0:T(8,128)(2,1)S(1)}, u32[]{:S(2)}, u32[]{:S(2)}) collective-permute-start(bf16[4,320,128]{2,1,0:T(8,128)(2,1)S(1)} %collective-permute-done.41.refs_1_), channel_id=1, source_target_pairs={{0,1},{1,0},{2,3},{3,2},{4,5},{5,4},{6,7},{7,6},{8,9},{9,8},{10,11... | collective-permute-start | bytes 983048 | tf_op jit(solution)/shard_map/ppermute | solution.py:1077
  228.5 4.5 %collective-permute-start.46 = (bf16[4,320,128]{2,1,0:T(8,128)(2,1)S(1)}, bf16[4,320,128]{2,1,0:T(8,128)(2,1)S(1)}, u32[]{:S(2)}, u32[]{:S(2)}) collective-permute-start(bf16[4,320,128]{2,1,0:T(8,128)(2,1)S(1)} %collective-permute-done.42.refs_2_), channel_id=1, source_target_pairs={{0,1},{1,0},{2,3},{3,2},{4,5},{5,4},{6,7},{7,6},{8,9},{9,8},{10,11... | collective-permute-start | bytes 983048 | tf_op jit(solution)/shard_map/ppermute | solution.py:1077
  228.5 4.5 %collective-permute-start.47 = (bf16[4,320,128]{2,1,0:T(8,128)(2,1)S(1)}, bf16[4,320,128]{2,1,0:T(8,128)(2,1)S(1)}, u32[]{:S(2)}, u32[]{:S(2)}) collective-permute-start(bf16[4,320,128]{2,1,0:T(8,128)(2,1)S(1)} %collective-permute-done.43.refs_3_), channel_id=1, source_target_pairs={{0,1},{1,0},{2,3},{3,2},{4,5},{5,4},{6,7},{7,6},{8,9},{9,8},{10,11... | collective-permute-start | bytes 983048 | tf_op jit(solution)/shard_map/ppermute | solution.py:1077
  (42 other events, 539.3 us)
Sparse Core Ops, SparseCore 0:
  34.0 77.2 all-gather.4
  116.1 55.2 all-gather.6
